TPU v7x, 32 devices: a whole 2x2x4 slice. The times are simulated.
32 devices in a mesh: seq: 4 (over y, x), expert: 4 (over z), mp: 2 (over core).
Axes of the slice: x: 2, y: 2, z: 4, core: 2. Of those that a mesh axis runs over, the one named last changes fastest.
Arguments:
- activations: bfloat16 [4096, 4096], P('seq', ('expert', 'mp')), may hold values from -6 to 6
- output_gradient: bfloat16 [4096, 4096], P('seq', ('expert', 'mp')), may hold values from -1.5 to 1.5
- input_state_map: bfloat16 [4096, 16], P('seq'), may hold values from -3 to 3
- output_state_map: bfloat16 [4096, 16], P('seq'), may hold values from -3 to 3
- head_decay_speed: float32 [64], P(('expert', 'mp')), may hold values from 1.2207031e-05 to 0.05, as said below
- spike_decay_level: int32 [4096], P('seq'), may hold values from 0 to 2, as said below
- assign: int32 [32], replicated, may hold values from 0 to 15, as said below
- expert_up_weight: bfloat16 [4, 4096, 12288], P('expert', 'mp', 'seq'), may hold values from -0.09375 to 0.09375
- expert_down_weight: bfloat16 [4, 12288, 4096], P('expert', 'seq', 'mp'), may hold values from -0.0546875 to 0.0546875
Outputs:
- grad_x: float32 [4096, 4096], P('seq', ('expert', 'mp'))
- grad_w_up: float32 [4, 4096, 12288], P('expert', 'mp', 'seq')
- grad_w_down: float32 [4, 12288, 4096], P('expert', 'seq', 'mp')
Inputs may be any that keep to these rules, and one draw needn't show every extreme that they name: `head_decay_speed`: some of the heads keep a tenth or more of their state over the whole sequence, the others lose it within some tens of tokens. `spike_decay_level`: at most three tokens of the sequence have a nonzero level. `assign`: numbers below 4 are the window's experts: the 8 blocks of one index of seq hold at most one block of each of them, each takes at most 2 blocks in all, and one takes exactly 2.
All inputs are finite; a program needn't handle non-finite values.
Results may differ from a plain program's by a relative error of at most 0.019.
Values may be sent and summed in bfloat16 or wider, within the bound.
A program may use at most 192 MiB of HBM per device.

v0:
```python
import jax
import jax.numpy as jnp
from jax import lax
from jax.sharding import PartitionSpec as P

HEAD = 64
STATE = 16
BLOCK = 128


spike_position_step = 0.3
highest = lax.Precision.HIGHEST


def from_behind(value, axis, steps):
    count = lax.axis_size(axis)
    first, last = (max(0, -steps), min(count, count - steps))
    return lax.ppermute(value, axis, [(source, source + steps) for source in range(first, last)])


def rounded(rounded_in):
    return lax.optimization_barrier(rounded_in.astype(jnp.bfloat16)).astype(jnp.float32)


def split_parts(values):
    high_part = values.astype(jnp.bfloat16)
    low_part = (values - high_part.astype(jnp.float32)).astype(jnp.bfloat16)
    return (high_part, low_part)


def mixing(cum_block, scores, causal):
    spread = cum_block.T[:, :, None] - cum_block.T[:, None, :]
    spread = jnp.where(causal[None], spread, -jnp.inf)
    return jnp.exp(spread) * scores[None]


def narrow(gathered, exp_index, mp_index, half_width):
    row_set = lax.dynamic_index_in_dim(gathered, exp_index, 0, keepdims=False)
    return lax.dynamic_slice_in_dim(row_set, mp_index * half_width, half_width, 1)


def compact(select, gathered, half_width):
    shaped = gathered.reshape(select.shape[1], -1, half_width)
    rows_out = jnp.einsum("js,srf->jrf", select, shaped, preferred_element_type=jnp.float32)
    return rows_out.astype(jnp.bfloat16).reshape(-1, half_width)


def per_device(
    activations,
    output_gradient,
    input_state_map,
    output_state_map,
    head_decay_speed,
    spike_decay_level,
    assign,
    expert_up_weight,
    expert_down_weight,
):
    tokens, slice_width = activations.shape
    heads_dev = slice_width // HEAD
    seq_count = lax.axis_size("seq")
    exp_count = lax.axis_size("expert")
    mp_count = lax.axis_size("mp")
    seq_index = lax.axis_index("seq")
    exp_index = lax.axis_index("expert")
    mp_index = lax.axis_index("mp")
    my_slice = exp_index * mp_count + mp_index
    slice_half = my_slice // exp_count
    half_width = slice_width * exp_count
    slot_total = seq_count // 2
    input_scale = jnp.sqrt(1.0 - jnp.exp(-2.0 * head_decay_speed))
    cum_level = jnp.cumsum(
        -head_decay_speed[None, :]
        - spike_position_step * spike_decay_level.astype(jnp.float32)[:, None],
        axis=0,
    )
    b_float = input_state_map.astype(jnp.float32)
    c_float = output_state_map.astype(jnp.float32)
    act_heads = activations.reshape(tokens, heads_dev, HEAD)
    scaled = act_heads.astype(jnp.float32) * input_scale[None, :, None]
    span_rows = min(512, tokens)
    span_count = tokens // span_rows
    causal = jnp.arange(span_rows)[:, None] >= jnp.arange(span_rows)[None, :]
    zero_level = jnp.zeros((heads_dev,), jnp.float32)
    carry_state = jnp.zeros((heads_dev, HEAD, STATE), jnp.float32)
    pieces = []
    for position in range(span_count):
        first_row = position * span_rows
        last_row = first_row + span_rows
        cum_block = cum_level[first_row:last_row]
        start_level = cum_level[first_row - 1] if position > 0 else zero_level
        scores = jnp.dot(
            output_state_map[first_row:last_row],
            input_state_map[first_row:last_row].T,
            preferred_element_type=jnp.float32,
        )
        weights = mixing(cum_block, scores, causal)
        weight_high, weight_low = split_parts(weights)
        x_span = act_heads[first_row:last_row]
        inner_part = jnp.einsum(
            "hts,shp->thp", weight_high, x_span, preferred_element_type=jnp.float32
        )
        inner_part = inner_part + jnp.einsum(
            "hts,shp->thp", weight_low, x_span, preferred_element_type=jnp.float32
        )
        inner_part = inner_part * input_scale[None, :, None]
        carried = jnp.exp(cum_block - start_level[None, :])[:, :, None] * jnp.einsum(
            "tn,hpn->thp", c_float[first_row:last_row], carry_state, precision=highest
        )
        pieces.append(inner_part + carried)
        end_level = cum_block[-1]
        tail_decay = jnp.exp(end_level[None, :] - cum_block)
        carry_state = jnp.exp(end_level - start_level)[:, None, None] * carry_state + jnp.einsum(
            "shp,sn->hpn",
            scaled[first_row:last_row] * tail_decay[:, :, None],
            b_float[first_row:last_row],
            precision=highest,
        )
    device_decay = jnp.exp(cum_level[-1])
    flat_state = carry_state.reshape(heads_dev, HEAD * STATE)

    def relay_state(rounds, carried_in):
        return from_behind(
            (device_decay[:, None] * carried_in + flat_state).astype(jnp.bfloat16), "seq", 1
        ).astype(jnp.float32)

    incoming = lax.fori_loop(0, seq_count - 1, relay_state, jnp.zeros_like(flat_state))
    incoming = incoming.reshape(heads_dev, HEAD, STATE)
    outputs = jnp.concatenate(pieces, axis=0) + jnp.exp(cum_level)[:, :, None] * jnp.einsum(
        "tn,hpn->thp", c_float, incoming, precision=highest
    )
    mixed_out = (activations.astype(jnp.float32) + outputs.reshape(tokens, slice_width)).astype(
        jnp.bfloat16
    )
    blocks_dev = tokens // BLOCK
    route_table = assign.reshape(seq_count, blocks_dev)
    own_row = lax.dynamic_index_in_dim(route_table, seq_index, 0, keepdims=False)
    chosen = (own_row[None, :] == jnp.arange(exp_count)[:, None]).astype(jnp.bfloat16)
    h_pick = jnp.einsum(
        "eb,brf->erf",
        chosen,
        mixed_out.reshape(blocks_dev, BLOCK, slice_width),
        preferred_element_type=jnp.float32,
    ).astype(jnp.bfloat16)
    g_pick = jnp.einsum(
        "eb,brf->erf",
        chosen,
        output_gradient.reshape(blocks_dev, BLOCK, slice_width),
        preferred_element_type=jnp.float32,
    ).astype(jnp.bfloat16)
    h_full, g_full = (
        lax.all_gather(h_pick, ("expert", "mp"), axis=2, tiled=True),
        lax.all_gather(g_pick, ("expert", "mp"), axis=2, tiled=True),
    )
    h_block = narrow(h_full, exp_index, mp_index, half_width)
    g_block = narrow(g_full, exp_index, mp_index, half_width)
    h_all, g_all = (
        lax.all_gather(h_block, "seq", axis=0, tiled=True),
        lax.all_gather(g_block, "seq", axis=0, tiled=True),
    )
    present = jnp.any(route_table == exp_index, axis=1)
    slot_of = jnp.cumsum(present.astype(jnp.int32)) - 1
    select = ((slot_of[None, :] == jnp.arange(slot_total)[:, None]) & present[None, :]).astype(
        jnp.bfloat16
    )
    x_rows = compact(select, h_all, half_width)
    g_rows = compact(select, g_all, half_width)
    up_local = expert_up_weight[0]
    down_local = expert_down_weight[0]
    pre_act = lax.psum(
        rounded(jnp.dot(x_rows, up_local, preferred_element_type=jnp.float32)).astype(jnp.bfloat16),
        "mp",
    ).astype(jnp.float32)
    activation = jax.nn.silu(pre_act).astype(jnp.bfloat16)
    down_grad = jnp.einsum("tf,td->fd", activation, g_rows, preferred_element_type=jnp.float32)
    act_grad = lax.psum(
        rounded(
            jnp.einsum("td,fd->tf", g_rows, down_local, preferred_element_type=jnp.float32)
        ).astype(jnp.bfloat16),
        "mp",
    ).astype(jnp.float32)
    sigmoid_pre = jax.nn.sigmoid(pre_act)
    pre_grad = (act_grad * sigmoid_pre * (1.0 + pre_act * (1.0 - sigmoid_pre))).astype(jnp.bfloat16)
    up_grad = jnp.einsum("td,tf->df", x_rows, pre_grad, preferred_element_type=jnp.float32)
    row_grad = jnp.einsum("tf,df->td", pre_grad, up_local, preferred_element_type=jnp.float32)
    row_grad = row_grad.astype(jnp.bfloat16).reshape(slot_total, BLOCK, half_width)
    spread_rows = jnp.einsum("js,jrf->srf", select, row_grad, preferred_element_type=jnp.float32)
    back_rows = lax.psum_scatter(
        spread_rows.reshape(BLOCK * lax.axis_size("seq"), half_width).astype(jnp.bfloat16),
        "seq",
        scatter_dimension=0,
        tiled=True,
    )
    arrived = lax.all_gather(back_rows[None], ("expert", "mp"), axis=0, tiled=True)
    halves = lax.dynamic_index_in_dim(
        arrived.reshape(exp_count, mp_count, BLOCK, half_width), slice_half, 1, keepdims=False
    )
    returned = lax.dynamic_slice_in_dim(halves, my_slice % exp_count * slice_width, slice_width, 2)
    token_grad = jnp.einsum("eb,erf->brf", chosen, returned, preferred_element_type=jnp.float32)
    total_grad = output_gradient.astype(jnp.float32) + token_grad.reshape(tokens, slice_width)
    grad_view = total_grad.reshape(tokens, heads_dev, HEAD)
    adjoint = jnp.zeros((heads_dev, HEAD, STATE), jnp.float32)
    back_pieces = [None] * span_count
    for position in reversed(range(span_count)):
        first_row = position * span_rows
        last_row = first_row + span_rows
        cum_block = cum_level[first_row:last_row]
        start_level = cum_level[first_row - 1] if position > 0 else zero_level
        scores = jnp.dot(
            output_state_map[first_row:last_row],
            input_state_map[first_row:last_row].T,
            preferred_element_type=jnp.float32,
        )
        weights = mixing(cum_block, scores, causal)
        weight_high, weight_low = split_parts(weights)
        grad_high, grad_low = split_parts(grad_view[first_row:last_row])
        inner_part = jnp.einsum(
            "hts,thp->shp", weight_high, grad_high, preferred_element_type=jnp.float32
        )
        inner_part = inner_part + jnp.einsum(
            "hts,thp->shp", weight_high, grad_low, preferred_element_type=jnp.float32
        )
        inner_part = inner_part + jnp.einsum(
            "hts,thp->shp", weight_low, grad_high, preferred_element_type=jnp.float32
        )
        end_level = cum_block[-1]
        tail_decay = jnp.exp(end_level[None, :] - cum_block)
        carried = tail_decay[:, :, None] * jnp.einsum(
            "sn,hpn->shp", b_float[first_row:last_row], adjoint, precision=highest
        )
        back_pieces[position] = inner_part + carried
        lead_decay = jnp.exp(cum_block - start_level[None, :])
        adjoint = jnp.exp(end_level - start_level)[:, None, None] * adjoint + jnp.einsum(
            "rhp,rn->hpn",
            grad_view[first_row:last_row] * lead_decay[:, :, None],
            c_float[first_row:last_row],
            precision=highest,
        )
    flat_adjoint = adjoint.reshape(heads_dev, HEAD * STATE)

    def relay_adjoint(rounds, carried_in):
        return from_behind(
            (device_decay[:, None] * carried_in + flat_adjoint).astype(jnp.bfloat16), "seq", -1
        ).astype(jnp.float32)

    later_adjoint = lax.fori_loop(0, seq_count - 1, relay_adjoint, jnp.zeros_like(flat_adjoint))
    later_adjoint = later_adjoint.reshape(heads_dev, HEAD, STATE)
    scan_grad = jnp.concatenate(back_pieces, axis=0) + jnp.exp(cum_level[-1][None, :] - cum_level)[
        :, :, None
    ] * jnp.einsum("sn,hpn->shp", b_float, later_adjoint, precision=highest)
    grad_x = total_grad + (input_scale[None, :, None] * scan_grad).reshape(tokens, slice_width)
    return (grad_x, up_grad[None], down_grad[None])


def solution(mesh):
    in_specs = (
        P("seq", ("expert", "mp")),
        P("seq", ("expert", "mp")),
        P("seq", None),
        P("seq", None),
        P(("expert", "mp")),
        P("seq"),
        P(),
        P("expert", "mp", "seq"),
        P("expert", "seq", "mp"),
    )
    out_specs = (P("seq", ("expert", "mp")), P("expert", "mp", "seq"), P("expert", "seq", "mp"))
    return jax.shard_map(
        per_device, mesh=mesh, in_specs=in_specs, out_specs=out_specs, check_vma=False
    )
```

profile of v0, /device:TPU:0, one launch (start us, length us, event | category | flops | bytes accessed | tf_op | source)
XLA Modules:
  0.0 398.7 jit_solution(4492388996279637979)
XLA Ops:
  8.6 2.8 convolution_convert_fusion.4
  12.9 2.3 reduce-window.19
  16.2 1.5 copy.132
  18.7 2.0 copy.130
  20.8 2.1 copy.131
  26.6 18.1 %while.22 = (s32[]{:T(128)}, f32[8,1024]{1,0:T(8,128)S(1)}, f32[8]{0:T(128)S(1)}, f32[8,1024]{1,0:T(8,128)S(1)}, s32[]{:T(128)}, /*index=5*/s32[]{:T(128)}) while((s32[]{:T(128)}, f32[8,1024]{1,0:T(8,128)S(1)}, f32[8]{0:T(128)S(1)}, f32[8,1024]{1,0:T(8,128)S(1)}, s32[]{:T(128)}, /*index=5*/s32[]{:T(128)}) %tuple.59), condition=%wide.region_6.7_spmd.clone, body=%wide.region_5.6_spmd.clone.sunk | while | flops 40963 | bytes 196759 | solution.py:127
  26.7 4.9 %collective-permute-start = (bf16[8,1024]{1,0:T(8,128)(2,1)S(1)}, bf16[8,1024]{1,0:T(8,128)(2,1)S(1)}, u32[]{:S(2)}, u32[]{:S(2)}) collective-permute-start(bf16[8,1024]{1,0:T(8,128)(2,1)S(1)} %fusion.200), channel_id=1, source_target_pairs={{0,8},{8,16},{16,24},{1,9},{9,17},{17,25},{2,10},{10,18},{18,26},{... | collective-permute-start | bytes 49160 | tf_op jit(solution)/shard_map/while/body/eval_jaxpr/ppermute | solution.py:18
  31.5 1.4 collective-permute-done
  33.0 4.2 %collective-permute-start = (bf16[8,1024]{1,0:T(8,128)(2,1)S(1)}, bf16[8,1024]{1,0:T(8,128)(2,1)S(1)}, u32[]{:S(2)}, u32[]{:S(2)}) collective-permute-start(bf16[8,1024]{1,0:T(8,128)(2,1)S(1)} %fusion.200), channel_id=1, source_target_pairs={{0,8},{8,16},{16,24},{1,9},{9,17},{17,25},{2,10},{10,18},{18,26},{... | collective-permute-start | bytes 49160 | tf_op jit(solution)/shard_map/while/body/eval_jaxpr/ppermute | solution.py:18
  37.2 1.4 collective-permute-done
  38.7 4.3 %collective-permute-start = (bf16[8,1024]{1,0:T(8,128)(2,1)S(1)}, bf16[8,1024]{1,0:T(8,128)(2,1)S(1)}, u32[]{:S(2)}, u32[]{:S(2)}) collective-permute-start(bf16[8,1024]{1,0:T(8,128)(2,1)S(1)} %fusion.200), channel_id=1, source_target_pairs={{0,8},{8,16},{16,24},{1,9},{9,17},{17,25},{2,10},{10,18},{18,26},{... | collective-permute-start | bytes 49160 | tf_op jit(solution)/shard_map/while/body/eval_jaxpr/ppermute | solution.py:18
  43.1 1.4 collective-permute-done
  45.4 1.4 subtract_exponential_fusion
  47.1 1.1 fusion.141
  48.2 4.0 %fusion.61 = f32[8,512,64]{1,2,0:T(8,128)S(1)} fusion(bf16[512,8,64]{0,2,1:T(8,128)(2,1)} %bitcast.178, f32[512,512]{1,0:T(8,128)S(1)} %fusion.148, f32[8,512]{1,0:T(8,128)} %get-tuple-element.114, pred[512,512]{1,0:T(8,128)(4,1)S(1)} %iota_compare_fusion), kind=kOutput, calls=%fused_computation.62 | convolution fusion | flops 283115520 | bytes 2899968 | tf_op jit(solution)/shard_map/hts,shp->thp/dot_general | solution.py:103
  52.3 2.4 fusion.109
  55.3 2.5 fusion.63
  57.9 2.4 fusion.97
  60.9 1.1 maximum_add_fusion
  62.0 2.0 copy.135
  64.0 1.9 add_convert_fusion
  66.0 1.5 convolution_convert_fusion.3
  67.6 3.5 constant_dynamic-slice_fusion.2
  71.1 1.1 copy.127
  72.3 47.0 %all-gather.11.cloned.1.call-done = bf16[4,128,4096]{2,0,1:T(4,128)(2,1)} async-done(((bf16[4,128,512]{2,0,1:T(4,128)(2,1)}), bf16[4,128,4096]{2,0,1:T(4,128)(2,1)}) %all-gather.11.cloned.1.call-update) | async-done | bytes 4194320 | tf_op jit(solution)/shard_map/all_gather | solution.py:152
  119.3 3.5 constant_dynamic-slice_fusion.1
  122.8 1.1 copy.137
  124.3 31.0 %all-gather.13.cloned.1.call-done = bf16[1,512,2048]{2,1,0:T(8,128)(2,1)} async-done(((bf16[1,128,2048]{2,1,0:T(8,128)(2,1)}), bf16[1,512,2048]{2,1,0:T(8,128)(2,1)}) %all-gather.13.cloned.1.call-update) | async-done | bytes 2097168 | tf_op jit(solution)/shard_map/all_gather | solution.py:159
  155.3 3.3 convolution_convert_fusion.2
  159.0 1.0 copy-done.11
  160.0 14.7 %fusion.54 = bf16[256,3072]{1,0:T(8,128)(2,1)} fusion(bf16[256,2048]{1,0:T(8,128)(2,1)S(1)} %bitcast.174, bf16[1,3072,2048]{2,1,0:T(8,128)(2,1)} %param.21), kind=kOutput, calls=%fused_computation.59 | convolution fusion | flops 3222011904 | bytes 15204352 | tf_op jit(solution)/shard_map/td,fd->tf/dot_general | solution.py:178
  174.7 18.3 %all-gather.15.cloned.1.call-done = bf16[1,512,2048]{2,1,0:T(8,128)(2,1)} async-done(((bf16[1,128,2048]{2,1,0:T(8,128)(2,1)}), bf16[1,512,2048]{2,1,0:T(8,128)(2,1)}) %all-gather.15.cloned.1.call-update) | async-done | bytes 2097168 | tf_op jit(solution)/shard_map/all_gather | solution.py:158
  192.9 3.3 convolution_convert_fusion.1
  196.6 9.1 %fusion.57 = bf16[256,3072]{1,0:T(8,128)(2,1)} fusion(bf16[256,2048]{1,0:T(8,128)(2,1)S(1)} %bitcast.162, bf16[1,2048,3072]{2,1,0:T(8,128)(2,1)} %param.20), kind=kOutput, calls=%fused_computation.60 | convolution fusion | flops 3222011904 | bytes 15204352 | tf_op jit(solution)/shard_map/dot_general | solution.py:171
  205.7 23.4 %all-reduce.3.cloned.1.call-done = (bf16[256,3072]{1,0:T(8,128)(2,1)}, bf16[256,3072]{1,0:T(8,128)(2,1)}) async-done(((bf16[256,3072]{1,0:T(8,128)(2,1)}, bf16[256,3072]{1,0:T(8,128)(2,1)}), (bf16[256,3072]{1,0:T(8,128)(2,1)}, bf16[256,3072]{1,0:T(8,128)(2,1)})) %all-reduce.3.cloned.1.call-update) | async-done | bytes 3145744 | tf_op jit(solution)/shard_map/psum | solution.py:170
  229.1 9.5 %fusion.71 = bf16[256,2048]{1,0:T(8,128)(2,1)S(1)} fusion(bf16[1,2048,3072]{2,1,0:T(8,128)(2,1)} %param.20, bf16[256,3072]{1,0:T(8,128)(2,1)} %get-tuple-element.97, bf16[256,3072]{1,0:T(8,128)(2,1)} %get-tuple-element.98), kind=kOutput, calls=%fused_computation.75 | convolution fusion | flops 3230400512 | bytes 16777216 | tf_op jit(solution)/shard_map/tf,df->td/dot_general | solution.py:185
  238.6 1.9 convolution_convert_fusion
  240.6 2.5 copy.141
  243.1 36.5 %reduce-scatter.2.cloned.1.call-done = bf16[128,2048]{1,0:T(8,128)(2,1)} async-done(((bf16[512,2048]{1,0:T(8,128)(2,1)}), bf16[128,2048]{1,0:T(8,128)(2,1)}) %reduce-scatter.2.cloned.1.call-update) | async-done | bytes 524304 | tf_op jit(solution)/shard_map/reduce_scatter | solution.py:188
  279.7 12.5 %convolution_bitcast_fusion.1 = f32[1,2048,3072]{2,1,0:T(8,128)} fusion(bf16[256,2048]{1,0:T(8,128)(2,1)S(1)} %bitcast.163, bf16[256,3072]{1,0:T(8,128)(2,1)S(1)} %copy-done.6, bf16[256,3072]{1,0:T(8,128)(2,1)} %get-tuple-element.98), kind=kOutput, calls=%fused_computation.7 | convolution fusion | flops 3229876224 | bytes 29360128 | tf_op jit(solution)/shard_map/td,tf->df/dot_general | solution.py:184
  292.2 10.8 %convolution_bitcast_fusion = f32[1,3072,2048]{2,1,0:T(8,128)} fusion(bf16[256,2048]{1,0:T(8,128)(2,1)S(1)} %bitcast.175, bf16[256,3072]{1,0:T(8,128)(2,1)S(1)} %copy-done.6), kind=kOutput, calls=%fused_computation.6 | convolution fusion | flops 3225944064 | bytes 27787264 | tf_op jit(solution)/shard_map/tf,td->fd/dot_general | solution.py:175
  303.0 25.4 %all-gather.17.cloned.1.call-done = bf16[1024,2048]{1,0:T(8,128)(2,1)} async-done(((bf16[128,2048]{1,0:T(8,128)(2,1)}), bf16[1024,2048]{1,0:T(8,128)(2,1)}) %all-gather.17.cloned.1.call-update) | async-done | bytes 4194320 | tf_op jit(solution)/shard_map/all_gather | solution.py:194
  328.4 1.3 constant_dynamic-slice_fusion
  330.3 1.2 copy.143
  332.0 1.5 fusion.183
  333.5 1.6 copy.144
  335.1 3.7 fusion.12
  338.8 2.3 fusion.112
  341.1 3.5 fusion.90
  344.6 1.6 copy.145
  346.3 4.7 %fusion.18 = f32[8,64,512]{2,1,0:T(8,128)} fusion(f32[512,512]{1,0:T(8,128)} %copy-done.7, f32[8,512]{1,0:T(8,128)} %get-tuple-element.113, pred[512,512]{1,0:T(8,128)(4,1)S(1)} %copy-done.23, f32[512,8,64]{0,2,1:T(8,128)S(1)} %bitcast.165), kind=kOutput, calls=%fused_computation.26 | convolution fusion | flops 277872640 | bytes 3424256 | tf_op jit(solution)/shard_map/hts,thp->shp/dot_general | solution.py:220
  352.0 1.4 convolution_add_fusion
  355.2 20.1 %while.23 = (s32[]{:T(128)}, f32[8,1024]{1,0:T(8,128)S(1)}, f32[8]{0:T(128)}, f32[8,1024]{1,0:T(8,128)S(1)}, s32[]{:T(128)}, /*index=5*/s32[]{:T(128)}) while((s32[]{:T(128)}, f32[8,1024]{1,0:T(8,128)S(1)}, f32[8]{0:T(128)}, f32[8,1024]{1,0:T(8,128)S(1)}, s32[]{:T(128)}, /*index=5*/s32[]{:T(128)}) %tuple.80), condition=%wide.region_10.11_spmd.clone, body=%wide.region_9.10_spmd.clone.sunk | while | flops 40963 | bytes 196759 | solution.py:246
  355.9 1.3 collective-permute-start.1
  357.2 4.3 %collective-permute-done.1 = bf16[8,1024]{1,0:T(8,128)(2,1)S(1)} collective-permute-done((bf16[8,1024]{1,0:T(8,128)(2,1)S(1)}, bf16[8,1024]{1,0:T(8,128)(2,1)S(1)}, u32[]{:S(2)}, u32[]{:S(2)}) %collective-permute-start.1) | collective-permute-done | bytes 16416 | tf_op jit(solution)/shard_map/while/body/eval_jaxpr/ppermute | solution.py:18
  362.2 1.3 collective-permute-start.1
  363.5 4.7 %collective-permute-done.1 = bf16[8,1024]{1,0:T(8,128)(2,1)S(1)} collective-permute-done((bf16[8,1024]{1,0:T(8,128)(2,1)S(1)}, bf16[8,1024]{1,0:T(8,128)(2,1)S(1)}, u32[]{:S(2)}, u32[]{:S(2)}) %collective-permute-start.1) | collective-permute-done | bytes 16416 | tf_op jit(solution)/shard_map/while/body/eval_jaxpr/ppermute | solution.py:18
  368.9 1.3 collective-permute-start.1
  370.1 5.2 %collective-permute-done.1 = bf16[8,1024]{1,0:T(8,128)(2,1)S(1)} collective-permute-done((bf16[8,1024]{1,0:T(8,128)(2,1)S(1)}, bf16[8,1024]{1,0:T(8,128)(2,1)S(1)}, u32[]{:S(2)}, u32[]{:S(2)}) %collective-permute-start.1) | collective-permute-done | bytes 16416 | tf_op jit(solution)/shard_map/while/body/eval_jaxpr/ppermute | solution.py:18
  375.5 4.2 %fusion.100 = f32[8,64,512]{2,1,0:T(8,128)S(1)} fusion(f32[8,64,512]{2,1,0:T(8,128)} %fusion.18, f32[512,512]{1,0:T(8,128)} %copy-done.7, f32[8,512]{1,0:T(8,128)} %get-tuple-element.113, pred[512,512]{1,0:T(8,128)(4,1)} %copy-done.22, f32[512,8,64]{0,2,1:T(8,128)} %bitcast.167), kind=kOutput, calls=%fused_computation.105 | convolution fusion | flops 277348352 | bytes 4472832 | tf_op jit(solution)/shard_map/hts,thp->shp/dot_general | solution.py:217
  379.8 2.5 fusion.88
  383.0 2.4 fusion.74
  385.4 2.9 copy.148
  388.3 3.4 add.166
  (159 shorter events, 19.0 us)
Async XLA Ops:
  7.2 10.5 %copy-start = (bf16[1024,512]{1,0:T(8,128)(2,1)S(1)}, bf16[1024,512]{1,0:T(8,128)(2,1)}, u32[]{:S(2)}) copy-start(bf16[1024,512]{1,0:T(8,128)(2,1)} %param.13) | copy-start | bytes 3145732
  7.2 60.4 %all-gather.9.cloned.1.call-start = ((), (), s32[]{:S(2)}) async-start(), calls=%async_computation.1 | async-start | bytes 4718592 | tf_op jit(solution)/shard_map/all_gather | solution.py:153
  8.0 4.8 %copy-start.38 = (s32[4,8]{1,0:T(4,128)}, s32[4,8]{1,0:T(4,128)S(1)}, u32[]{:S(2)}) copy-start(s32[4,8]{1,0:T(4,128)S(1)} %reshape.164) | copy-start | bytes 388
  8.1 0.6 copy-start.40
  11.4 107.9 %all-gather.11.cloned.1.call-start = ((), (), s32[]{:S(2)}) async-start(), calls=%async_computation.2 | async-start | bytes 4718592 | tf_op jit(solution)/shard_map/all_gather | solution.py:152
  12.1 12.5 %copy-start.42 = (f32[8]{0:T(128)}, f32[8]{0:T(128)S(1)}, u32[]{:S(2)}) copy-start(f32[8]{0:T(128)S(1)} %get-tuple-element.120) | copy-start | bytes 100
  15.6 0.6 copy-start.20
  17.7 7.0 %copy-start.15 = (bf16[1024,16]{0,1:T(8,128)(2,1)S(1)}, bf16[1024,16]{0,1:T(8,128)(2,1)}, u32[]{:S(2)}) copy-start(bf16[1024,16]{0,1:T(8,128)(2,1)} %param.15) | copy-start | bytes 98308
  23.1 2.4 copy-start.37
  24.4 1.1 copy-start.25
  24.4 22.4 %copy-start.14 = (bf16[1024,16]{0,1:T(8,128)(2,1)S(1)}, bf16[1024,16]{0,1:T(8,128)(2,1)}, u32[]{:S(2)}) copy-start(bf16[1024,16]{0,1:T(8,128)(2,1)} %param.16) | copy-start | bytes 98308
  24.7 20.7 %copy-start.21 = (f32[1,8,8,128]{3,2,1,0:T(8,128)S(1)}, f32[1,8,8,128]{3,2,1,0:T(8,128)}, u32[]{:S(2)}) copy-start(f32[1,8,8,128]{3,2,1,0:T(8,128)} %copy-done.20) | copy-start | bytes 98308
  24.7 22.1 %copy-start.16 = (bf16[1024,16]{0,1:T(8,128)(2,1)S(1)}, bf16[1024,16]{0,1:T(8,128)(2,1)}, u32[]{:S(2)}) copy-start(bf16[1024,16]{0,1:T(8,128)(2,1)} %param.15) | copy-start | bytes 98308
  26.7 6.3 %collective-permute-start = (bf16[8,1024]{1,0:T(8,128)(2,1)S(1)}, bf16[8,1024]{1,0:T(8,128)(2,1)S(1)}, u32[]{:S(2)}, u32[]{:S(2)}) collective-permute-start(bf16[8,1024]{1,0:T(8,128)(2,1)S(1)} %fusion.200), channel_id=1, source_target_pairs={{0,8},{8,16},{16,24},{1,9},{9,17},{17,25},{2,10},{10,18},{18,26},{... | collective-permute-start | bytes 49160 | tf_op jit(solution)/shard_map/while/body/eval_jaxpr/ppermute | solution.py:18
  33.0 5.6 %collective-permute-start = (bf16[8,1024]{1,0:T(8,128)(2,1)S(1)}, bf16[8,1024]{1,0:T(8,128)(2,1)S(1)}, u32[]{:S(2)}, u32[]{:S(2)}) collective-permute-start(bf16[8,1024]{1,0:T(8,128)(2,1)S(1)} %fusion.200), channel_id=1, source_target_pairs={{0,8},{8,16},{16,24},{1,9},{9,17},{17,25},{2,10},{10,18},{18,26},{... | collective-permute-start | bytes 49160 | tf_op jit(solution)/shard_map/while/body/eval_jaxpr/ppermute | solution.py:18
  38.7 5.7 %collective-permute-start = (bf16[8,1024]{1,0:T(8,128)(2,1)S(1)}, bf16[8,1024]{1,0:T(8,128)(2,1)S(1)}, u32[]{:S(2)}, u32[]{:S(2)}) collective-permute-start(bf16[8,1024]{1,0:T(8,128)(2,1)S(1)} %fusion.200), channel_id=1, source_target_pairs={{0,8},{8,16},{16,24},{1,9},{9,17},{17,25},{2,10},{10,18},{18,26},{... | collective-permute-start | bytes 49160 | tf_op jit(solution)/shard_map/while/body/eval_jaxpr/ppermute | solution.py:18
  44.6 0.5 copy-start.32
  45.4 12.5 %copy-start.22 = (pred[512,512]{1,0:T(8,128)(4,1)}, pred[512,512]{1,0:T(8,128)(4,1)S(1)}, u32[]{:S(2)}) copy-start(pred[512,512]{1,0:T(8,128)(4,1)S(1)} %iota_compare_fusion) | copy-start | bytes 786436
  47.1 5.1 %copy-start.9 = (f32[512,512]{1,0:T(8,128)}, f32[512,512]{1,0:T(8,128)S(1)}, u32[]{:S(2)}) copy-start(f32[512,512]{1,0:T(8,128)S(1)} %fusion.148) | copy-start | bytes 3145732
  48.1 9.7 %copy-start.7 = (f32[512,512]{1,0:T(8,128)}, f32[512,512]{1,0:T(8,128)S(1)}, u32[]{:S(2)}) copy-start(f32[512,512]{1,0:T(8,128)S(1)} %fusion.141) | copy-start | bytes 3145732
  48.2 4.1 %copy-start.19 = (bf16[512,512]{0,1:T(8,128)(2,1)S(1)}, bf16[512,512]{0,1:T(8,128)(2,1)}, u32[]{:S(2)}) copy-start(bf16[512,512]{0,1:T(8,128)(2,1)} %copy.130) | copy-start | bytes 1572868
  48.2 4.1 %copy-start.35 = (f32[8,512]{1,0:T(8,128)S(1)}, f32[8,512]{1,0:T(8,128)}, u32[]{:S(2)}) copy-start(f32[8,512]{1,0:T(8,128)} %get-tuple-element.114) | copy-start | bytes 49156
  48.2 4.1 %copy-start.43 = (f32[8]{0:T(128)S(1)}, f32[8]{0:T(128)}, u32[]{:S(2)}) copy-start(f32[8]{0:T(128)} %copy-done.42) | copy-start | bytes 100
  52.3 2.4 copy-start.27
  52.3 3.0 copy-start.18
  52.3 3.0 copy-start.33
  57.9 2.4 copy-start.29
  62.0 4.0 copy-start.41
  67.5 87.8 %all-gather.13.cloned.1.call-start = ((), (), s32[]{:S(2)}) async-start(), calls=%async_computation.4 | async-start | bytes 2621440 | tf_op jit(solution)/shard_map/all_gather | solution.py:159
  67.6 56.3 %copy-start.39 = (s32[4,8]{1,0:T(4,128)S(1)}, s32[4,8]{1,0:T(4,128)}, u32[]{:S(2)}) copy-start(s32[4,8]{1,0:T(4,128)} %copy-done.38) | copy-start | bytes 388
  72.2 120.7 %all-gather.15.cloned.1.call-start = ((), (), s32[]{:S(2)}) async-start(), calls=%async_computation.5 | async-start | bytes 2621440 | tf_op jit(solution)/shard_map/all_gather | solution.py:158
  123.9 105.2 %all-reduce.3.cloned.1.call-start = ((), (), s32[]{:S(2)}) async-start(), calls=%async_computation.7 | async-start | bytes 6291456 | tf_op jit(solution)/shard_map/psum | solution.py:170
  159.0 1.0 copy-start.11
  205.7 73.9 %reduce-scatter.2.cloned.1.call-start = ((), (), s32[]{:S(2)}) async-start(), calls=%async_computation.3 | async-start | bytes 2621440 | tf_op jit(solution)/shard_map/reduce_scatter | solution.py:188
  240.6 39.1 %copy-start.6 = (bf16[256,3072]{1,0:T(8,128)(2,1)S(1)}, bf16[256,3072]{1,0:T(8,128)(2,1)}, u32[]{:S(2)}) copy-start(bf16[256,3072]{1,0:T(8,128)(2,1)} %get-tuple-element.97) | copy-start | bytes 4718596
  243.1 85.3 %all-gather.17.cloned.1.call-start = ((), (), s32[]{:S(2)}) async-start(), calls=%async_computation.6 | async-start | bytes 4718592 | tf_op jit(solution)/shard_map/all_gather | solution.py:194
  279.7 12.5 %copy-start.12 = (bf16[2,128,2048]{2,1,0:T(8,128)(2,1)S(1)}, bf16[2,128,2048]{2,1,0:T(8,128)(2,1)}, u32[]{:S(2)}) copy-start(bf16[2,128,2048]{2,1,0:T(8,128)(2,1)} %copy-done.11) | copy-start | bytes 3145732
  303.0 28.5 %copy-start.1 = (bf16[1024,512]{1,0:T(8,128)(2,1)S(1)}, bf16[1024,512]{1,0:T(8,128)(2,1)}, u32[]{:S(2)}) copy-start(bf16[1024,512]{1,0:T(8,128)(2,1)} %param.14) | copy-start | bytes 3145732
  331.9 3.1 copy-start.23
  332.0 3.1 copy-start.36
  335.0 6.0 %copy-start.4 = (f32[512,512]{0,1:T(8,128)}, f32[512,512]{0,1:T(8,128)S(1)}, u32[]{:S(2)}) copy-start(f32[512,512]{0,1:T(8,128)S(1)} %copy.144) | copy-start | bytes 3145732
  335.1 3.7 copy-start.10
  346.2 4.8 %copy-start.2 = (f32[512,512]{0,1:T(8,128)}, f32[512,512]{0,1:T(8,128)S(1)}, u32[]{:S(2)}) copy-start(f32[512,512]{0,1:T(8,128)S(1)} %copy.145) | copy-start | bytes 3145732
  346.2 4.8 %copy-start.30 = (f32[512,8]{0,1:T(8,128)S(1)}, f32[512,8]{0,1:T(8,128)}, u32[]{:S(2)}) copy-start(f32[512,8]{0,1:T(8,128)} %get-tuple-element.112) | copy-start | bytes 49156
  346.2 4.8 %copy-start.46 = (f32[8]{0:T(128)S(1)}, f32[8]{0:T(128)}, u32[]{:S(2)}) copy-start(f32[8]{0:T(128)} %get-tuple-element.117) | copy-start | bytes 100
  346.2 5.8 %copy-start.5 = (f32[512,512]{0,1:T(8,128)S(1)}, f32[512,512]{0,1:T(8,128)}, u32[]{:S(2)}) copy-start(f32[512,512]{0,1:T(8,128)} %copy-done.4) | copy-start | bytes 3145732
  346.2 5.8 %copy-start.28 = (f32[512,8]{0,1:T(8,128)S(1)}, f32[512,8]{0,1:T(8,128)}, u32[]{:S(2)}) copy-start(f32[512,8]{0,1:T(8,128)} %get-tuple-element.110) | copy-start | bytes 49156
  346.2 5.8 %copy-start.45 = (f32[8]{0:T(128)S(1)}, f32[8]{0:T(128)}, u32[]{:S(2)}) copy-start(f32[8]{0:T(128)} %get-tuple-element.115) | copy-start | bytes 100
  346.2 7.2 %copy-start.13 = (f32[512,8,64]{0,2,1:T(8,128)S(1)}, f32[512,8,64]{0,2,1:T(8,128)}, u32[]{:S(2)}) copy-start(f32[512,8,64]{0,2,1:T(8,128)} %fusion.90) | copy-start | bytes 3145732
  346.2 7.2 %copy-start.17 = (bf16[1024,16]{0,1:T(8,128)(2,1)S(1)}, bf16[1024,16]{0,1:T(8,128)(2,1)}, u32[]{:S(2)}) copy-start(bf16[1024,16]{0,1:T(8,128)(2,1)} %param.15) | copy-start | bytes 98308
  346.3 7.2 %copy-start.26 = (f32[512,8]{0,1:T(8,128)S(1)}, f32[512,8]{0,1:T(8,128)}, u32[]{:S(2)}) copy-start(f32[512,8]{0,1:T(8,128)} %copy-done.25) | copy-start | bytes 49156
  355.9 5.6 %collective-permute-start.1 = (bf16[8,1024]{1,0:T(8,128)(2,1)S(1)}, bf16[8,1024]{1,0:T(8,128)(2,1)S(1)}, u32[]{:S(2)}, u32[]{:S(2)}) collective-permute-start(bf16[8,1024]{1,0:T(8,128)(2,1)S(1)} %fusion.201), channel_id=1, source_target_pairs={{8,0},{16,8},{24,16},{9,1},{17,9},{25,17},{10,2},{18,10},{26,18},{... | collective-permute-start | bytes 49160 | tf_op jit(solution)/shard_map/while/body/eval_jaxpr/ppermute | solution.py:18
  362.2 6.0 %collective-permute-start.1 = (bf16[8,1024]{1,0:T(8,128)(2,1)S(1)}, bf16[8,1024]{1,0:T(8,128)(2,1)S(1)}, u32[]{:S(2)}, u32[]{:S(2)}) collective-permute-start(bf16[8,1024]{1,0:T(8,128)(2,1)S(1)} %fusion.201), channel_id=1, source_target_pairs={{8,0},{16,8},{24,16},{9,1},{17,9},{25,17},{10,2},{18,10},{26,18},{... | collective-permute-start | bytes 49160 | tf_op jit(solution)/shard_map/while/body/eval_jaxpr/ppermute | solution.py:18
  368.9 6.5 %collective-permute-start.1 = (bf16[8,1024]{1,0:T(8,128)(2,1)S(1)}, bf16[8,1024]{1,0:T(8,128)(2,1)S(1)}, u32[]{:S(2)}, u32[]{:S(2)}) collective-permute-start(bf16[8,1024]{1,0:T(8,128)(2,1)S(1)} %fusion.201), channel_id=1, source_target_pairs={{8,0},{16,8},{24,16},{9,1},{17,9},{25,17},{10,2},{18,10},{26,18},{... | collective-permute-start | bytes 49160 | tf_op jit(solution)/shard_map/while/body/eval_jaxpr/ppermute | solution.py:18
  375.5 4.3 %copy-start.3 = (f32[512,512]{0,1:T(8,128)S(1)}, f32[512,512]{0,1:T(8,128)}, u32[]{:S(2)}) copy-start(f32[512,512]{0,1:T(8,128)} %copy-done.2) | copy-start | bytes 3145732
  375.5 4.3 %copy-start.8 = (f32[512,512]{1,0:T(8,128)S(1)}, f32[512,512]{1,0:T(8,128)}, u32[]{:S(2)}) copy-start(f32[512,512]{1,0:T(8,128)} %copy-done.7) | copy-start | bytes 3145732
  375.5 4.3 %copy-start.24 = (pred[512,512]{1,0:T(8,128)(4,1)S(1)}, pred[512,512]{1,0:T(8,128)(4,1)}, u32[]{:S(2)}) copy-start(pred[512,512]{1,0:T(8,128)(4,1)} %copy-done.22) | copy-start | bytes 786436
  375.5 4.3 %copy-start.34 = (f32[8,512]{1,0:T(8,128)S(1)}, f32[8,512]{1,0:T(8,128)}, u32[]{:S(2)}) copy-start(f32[8,512]{1,0:T(8,128)} %get-tuple-element.113) | copy-start | bytes 49156
  379.8 3.2 copy-start.31
  379.8 3.2 copy-start.44
Sparse Core Ops, SparseCore 0:
  11.5 50.5 all-gather.8
  67.7 51.6 all-gather.10
  121.7 33.5 all-gather.12
  157.6 35.3 all-gather.14
  205.8 23.2 all-reduce.2
  243.2 36.3 reduce-scatter.1
  281.2 47.1 all-gather.16
where the time goes:
time: 403 us; the launch traced here: 399 us
  waiting for transfers between devices  200 us (50%)
  matrix products  113 us (28%)
  local copies, waits for them, and re-layouts  36.8 us (9%)
  starting transfers between devices  17.5 us (4%)
  between operations  15.3 us (4%)
  other arithmetic  15.2 us (4%)
    all_gather x1, waiting for transfers between devices, per_device(): lax.all_gather(h_pick, ('expert', 'mp'), axis=2, tiled=True)  47 us
    reduce_scatter x1, waiting for transfers between devices, per_device(): lax.psum_scatter(spread_rows.reshape(BLOCK * lax.axis_size('seq'), half_w...  36.5 us
    all_gather x1, waiting for transfers between devices, per_device(): lax.all_gather(g_block, 'seq', axis=0, tiled=True)  31 us
    all_gather x1, waiting for transfers between devices, per_device(): lax.all_gather(back_rows[None], ('expert', 'mp'), axis=0, tiled=True)  25.4 us
    psum x1, waiting for transfers between devices, per_device(): lax.psum(rounded(jnp.dot(x_rows, up_local, preferred_element_type=jnp.flo...  23.4 us
    ppermute x6, waiting for transfers between devices, from_behind(): lax.ppermute(value, axis, [(source, source + steps) for source in range(f...  18.5 us
    all_gather x1, waiting for transfers between devices, per_device(): lax.all_gather(h_block, 'seq', axis=0, tiled=True)  18.3 us
    ppermute x6, starting transfers between devices, from_behind(): lax.ppermute(value, axis, [(source, source + steps) for source in range(f...  17.2 us
  transfers between devices with their start and end apart: 13, of which 12 were waited for; matrix products, arithmetic and copies ran while one was open for 22% of the time, Pallas kernels for 0%

commit v1 on v0

--- a/solution.py
+++ b/solution.py
@@ -1,6 +1,9 @@
+import functools
 import jax
 import jax.numpy as jnp
 from jax import lax
+from jax.experimental import pallas as pl
+from jax.experimental.pallas import tpu as pltpu
 from jax.sharding import PartitionSpec as P
 
 HEAD = 64
@@ -12,14 +15,280 @@
 highest = lax.Precision.HIGHEST
 
 
-def from_behind(value, axis, steps):
-    count = lax.axis_size(axis)
-    first, last = (max(0, -steps), min(count, count - steps))
-    return lax.ppermute(value, axis, [(source, source + steps) for source in range(first, last)])
-
-
-def rounded(rounded_in):
-    return lax.optimization_barrier(rounded_in.astype(jnp.bfloat16)).astype(jnp.float32)
+MESH = pl.DeviceIdType.MESH
+
+
+def place():
+    return (lax.axis_index("seq"), lax.axis_index("expert"), lax.axis_index("mp"))
+
+
+def greet_seq(n_seq, me):
+    s, e, m = me
+    barrier = pltpu.get_barrier_semaphore()
+    for step in range(1, n_seq):
+        pl.semaphore_signal(
+            barrier, inc=1, device_id=(lax.rem(s + step, n_seq), e, m), device_id_type=MESH
+        )
+    return barrier
+
+
+def share_kernel(n_seq, x_ref, out_ref, send_sem, recv_sem):
+    s, e, m = place()
+    barrier = greet_seq(n_seq, (s, e, m))
+    pl.semaphore_wait(barrier, n_seq - 1)
+    copies = []
+    for step in range(1, n_seq):
+        copy = pltpu.make_async_remote_copy(
+            src_ref=x_ref,
+            dst_ref=out_ref.at[s],
+            send_sem=send_sem.at[step],
+            recv_sem=recv_sem.at[step],
+            device_id=(lax.rem(s + step, n_seq), e, m),
+            device_id_type=MESH,
+        )
+        copy.start()
+        copies.append(copy)
+    out_ref[s] = x_ref[...]
+    for copy in copies:
+        copy.wait()
+
+
+def share(value, n_seq, collective_id):
+    return pl.pallas_call(
+        functools.partial(share_kernel, n_seq),
+        out_shape=jax.ShapeDtypeStruct((n_seq,) + value.shape, value.dtype),
+        in_specs=[pl.BlockSpec(memory_space=pltpu.VMEM)],
+        out_specs=pl.BlockSpec(memory_space=pltpu.VMEM),
+        scratch_shapes=[pltpu.SemaphoreType.DMA((n_seq,)), pltpu.SemaphoreType.DMA((n_seq,))],
+        compiler_params=pltpu.CompilerParams(collective_id=collective_id, has_side_effects=True),
+    )(value)
+
+
+def greet_all(n_seq, n_exp, n_mp, me, sources):
+    s, e, m = me
+    barrier = greet_seq(n_seq, me)
+    f = e * n_mp + m
+    own_half = f // n_exp == m
+    for i in range(n_exp):
+        for step in range(n_seq):
+            if sources:
+                part = m * n_exp + lax.rem(lax.rem(f, n_exp) + i, n_exp)
+                device = (lax.rem(s + step, n_seq), part // n_mp, lax.rem(part, n_mp))
+            else:
+                device = (lax.rem(s + step, n_seq), lax.rem(e + i, n_exp), f // n_exp)
+            if i == 0 and step == 0:
+
+                @pl.when(jnp.logical_not(own_half))
+                def _():
+                    pl.semaphore_signal(barrier, inc=1, device_id=device, device_id_type=MESH)
+            else:
+                pl.semaphore_signal(barrier, inc=1, device_id=device, device_id_type=MESH)
+    pl.semaphore_wait(barrier, n_seq * n_exp + n_seq - 1 - own_half.astype(jnp.int32))
+
+
+def scatter_copies(n_seq, n_exp, me, device_of, src_of, dst, send_sem, recv_sem, own_half):
+    pending = []
+    for i in range(n_exp):
+        for step in range(n_seq):
+            source, device = src_of(i, step), device_of(i, step)
+            copy = pltpu.make_async_remote_copy(
+                src_ref=source,
+                dst_ref=dst,
+                send_sem=send_sem.at[i, step],
+                recv_sem=recv_sem,
+                device_id=device,
+                device_id_type=MESH,
+            )
+            if i == 0 and step == 0:
+                local = pltpu.make_async_copy(source, dst, recv_sem)
+
+                @pl.when(own_half)
+                def _():
+                    local.start()
+
+                @pl.when(jnp.logical_not(own_half))
+                def _():
+                    copy.start()
+            else:
+                copy.start()
+            pending.append(copy)
+
+    def finish():
+        @pl.when(jnp.logical_not(own_half))
+        def _():
+            pending[0].wait_send()
+
+        for copy in pending[1:]:
+            copy.wait_send()
+
+    return finish
+
+
+def route_kernel(sizes, sel_ref, h_ref, g_ref, hx_ref, gx_ref, h_in, g_in, send_sem, recv_sem, sem_a, sem_b):
+    n_seq, n_exp, n_mp, slots = sizes
+    me = place()
+    s, e, m = me
+    f = e * n_mp + m
+    own_half = f // n_exp == m
+    width = h_ref.shape[-1]
+    greet_all(n_seq, n_exp, n_mp, me, True)
+
+    def device_of(i, step):
+        return (lax.rem(s + step, n_seq), lax.rem(e + i, n_exp), f // n_exp)
+
+    finishers = []
+    for k, (ref, landing) in enumerate(((g_ref, g_in), (h_ref, h_in))):
+        finishers.append(
+            scatter_copies(
+                n_seq,
+                n_exp,
+                me,
+                device_of,
+                lambda i, step, ref=ref: ref.at[lax.rem(e + i, n_exp), lax.rem(s + step, n_seq)],
+                landing.at[s, lax.rem(f, n_exp)],
+                send_sem.at[k],
+                recv_sem.at[k],
+                own_half,
+            )
+        )
+    copies = []
+    for k, (landing, out) in enumerate(((g_in, gx_ref), (h_in, hx_ref))):
+        pltpu.make_async_copy(landing, landing, recv_sem.at[k]).wait()
+        for j in range(slots):
+            for q in range(n_exp):
+                total = sel_ref[j, 0] * landing[0, q].astype(jnp.float32)
+                for source in range(1, n_seq):
+                    total = total + sel_ref[j, source] * landing[source, q].astype(jnp.float32)
+                out[s, j, :, q * width : (q + 1) * width] = total.astype(jnp.bfloat16)
+        for step in range(1, n_seq):
+            copy = pltpu.make_async_remote_copy(
+                src_ref=out.at[s],
+                dst_ref=out.at[s],
+                send_sem=sem_a.at[k, step],
+                recv_sem=sem_b.at[k, step],
+                device_id=(lax.rem(s + step, n_seq), e, m),
+                device_id_type=MESH,
+            )
+            copy.start()
+            copies.append(copy)
+    for copy in copies:
+        copy.wait()
+    for finish in finishers:
+        finish()
+
+
+def route(select, h_pick, g_pick, sizes):
+    n_seq, n_exp, n_mp, slots = sizes
+    width = h_pick.shape[-1]
+    part = BLOCK // n_seq
+    picks = [v.reshape(n_exp, n_seq, part, width) for v in (h_pick, g_pick)]
+    out = jax.ShapeDtypeStruct((n_seq, slots, part, width * n_exp), jnp.bfloat16)
+    vmem = pl.BlockSpec(memory_space=pltpu.VMEM)
+    return pl.pallas_call(
+        functools.partial(route_kernel, sizes),
+        out_shape=(out, out),
+        in_specs=[pl.BlockSpec(memory_space=pltpu.SMEM), vmem, vmem],
+        out_specs=(vmem, vmem),
+        scratch_shapes=[
+            pltpu.VMEM((n_seq, n_exp, part, width), jnp.bfloat16),
+            pltpu.VMEM((n_seq, n_exp, part, width), jnp.bfloat16),
+            pltpu.SemaphoreType.DMA((2, n_exp, n_seq)),
+            pltpu.SemaphoreType.DMA((2,)),
+            pltpu.SemaphoreType.DMA((2, n_seq)),
+            pltpu.SemaphoreType.DMA((2, n_seq)),
+        ],
+        compiler_params=pltpu.CompilerParams(
+            collective_id=1, has_side_effects=True, vmem_limit_bytes=40 * 2**20
+        ),
+    )(select, *picks)
+
+
+def unroute_kernel(sizes, sel_ref, r_ref, out_ref, r_in, spread, send_sem, recv_sem, sem_a, sem_b):
+    n_seq, n_exp, n_mp, slots = sizes
+    me = place()
+    s, e, m = me
+    f = e * n_mp + m
+    own_half = f // n_exp == m
+    width = out_ref.shape[-1]
+    greet_all(n_seq, n_exp, n_mp, me, False)
+    copies = []
+    for step in range(1, n_seq):
+        target = lax.rem(s + step, n_seq)
+        copy = pltpu.make_async_remote_copy(
+            src_ref=r_ref.at[target],
+            dst_ref=r_in.at[step - 1],
+            send_sem=sem_a.at[step],
+            recv_sem=sem_b.at[step],
+            device_id=(target, e, m),
+            device_id_type=MESH,
+        )
+        copy.start()
+        copies.append(copy)
+    for copy in copies:
+        copy.wait()
+    for q in range(n_exp):
+        totals = []
+        for j in range(slots):
+            cut = slice(q * width, (q + 1) * width)
+            total = r_ref[s, j, :, cut].astype(jnp.float32)
+            for step in range(n_seq - 1):
+                total = total + r_in[step, j, :, cut].astype(jnp.float32)
+            totals.append(total)
+        for source in range(n_seq):
+            row = sel_ref[0, source] * totals[0]
+            for j in range(1, slots):
+                row = row + sel_ref[j, source] * totals[j]
+            spread[source, q] = row.astype(jnp.bfloat16)
+
+    def part_of(i):
+        return lax.rem(lax.rem(f, n_exp) + i, n_exp)
+
+    def device_of(i, step):
+        part = m * n_exp + part_of(i)
+        return (lax.rem(s + step, n_seq), part // n_mp, lax.rem(part, n_mp))
+
+    finish = scatter_copies(
+        n_seq,
+        n_exp,
+        me,
+        device_of,
+        lambda i, step: spread.at[lax.rem(s + step, n_seq), part_of(i)],
+        out_ref.at[e, s],
+        send_sem,
+        recv_sem.at[0],
+        own_half,
+    )
+    pltpu.make_async_copy(out_ref, out_ref, recv_sem.at[0]).wait()
+    finish()
+
+
+def unroute(select, rows, sizes):
+    n_seq, n_exp, n_mp, slots = sizes
+    part = BLOCK // n_seq
+    half_width = rows.shape[-1]
+    width = half_width // n_exp
+    vmem = pl.BlockSpec(memory_space=pltpu.VMEM)
+    return pl.pallas_call(
+        functools.partial(unroute_kernel, sizes),
+        out_shape=jax.ShapeDtypeStruct((n_exp, n_seq, part, width), jnp.bfloat16),
+        in_specs=[pl.BlockSpec(memory_space=pltpu.SMEM), vmem],
+        out_specs=vmem,
+        scratch_shapes=[
+            pltpu.VMEM((n_seq - 1, slots, part, half_width), jnp.bfloat16),
+            pltpu.VMEM((n_seq, n_exp, part, width), jnp.bfloat16),
+            pltpu.SemaphoreType.DMA((n_exp, n_seq)),
+            pltpu.SemaphoreType.DMA((1,)),
+            pltpu.SemaphoreType.DMA((n_seq,)),
+            pltpu.SemaphoreType.DMA((n_seq,)),
+        ],
+        compiler_params=pltpu.CompilerParams(
+            collective_id=2, has_side_effects=True, vmem_limit_bytes=40 * 2**20
+        ),
+    )(select, rows.reshape(n_seq, slots, part, half_width))
+
+
+def swapped(value):
+    return lax.ppermute(value, "mp", [(0, 1), (1, 0)])
 
 
 def split_parts(values):
@@ -32,17 +301,6 @@
     spread = cum_block.T[:, :, None] - cum_block.T[:, None, :]
     spread = jnp.where(causal[None], spread, -jnp.inf)
     return jnp.exp(spread) * scores[None]
-
-
-def narrow(gathered, exp_index, mp_index, half_width):
-    row_set = lax.dynamic_index_in_dim(gathered, exp_index, 0, keepdims=False)
-    return lax.dynamic_slice_in_dim(row_set, mp_index * half_width, half_width, 1)
-
-
-def compact(select, gathered, half_width):
-    shaped = gathered.reshape(select.shape[1], -1, half_width)
-    rows_out = jnp.einsum("js,srf->jrf", select, shaped, preferred_element_type=jnp.float32)
-    return rows_out.astype(jnp.bfloat16).reshape(-1, half_width)
 
 
 def per_device(
@@ -63,16 +321,18 @@
     mp_count = lax.axis_size("mp")
     seq_index = lax.axis_index("seq")
     exp_index = lax.axis_index("expert")
-    mp_index = lax.axis_index("mp")
-    my_slice = exp_index * mp_count + mp_index
-    slice_half = my_slice // exp_count
     half_width = slice_width * exp_count
     slot_total = seq_count // 2
     input_scale = jnp.sqrt(1.0 - jnp.exp(-2.0 * head_decay_speed))
-    cum_level = jnp.cumsum(
-        -head_decay_speed[None, :]
-        - spike_position_step * spike_decay_level.astype(jnp.float32)[:, None],
-        axis=0,
+    row = jnp.arange(tokens)
+    spike_count = jnp.dot(
+        (row[:, None] >= row[None, :]).astype(jnp.bfloat16),
+        spike_decay_level.astype(jnp.bfloat16)[:, None],
+        preferred_element_type=jnp.float32,
+    )
+    cum_level = (
+        -(row + 1).astype(jnp.float32)[:, None] * head_decay_speed[None, :]
+        - spike_position_step * spike_count
     )
     b_float = input_state_map.astype(jnp.float32)
     c_float = output_state_map.astype(jnp.float32)
@@ -116,15 +376,31 @@
             b_float[first_row:last_row],
             precision=highest,
         )
-    device_decay = jnp.exp(cum_level[-1])
     flat_state = carry_state.reshape(heads_dev, HEAD * STATE)
-
-    def relay_state(rounds, carried_in):
-        return from_behind(
-            (device_decay[:, None] * carried_in + flat_state).astype(jnp.bfloat16), "seq", 1
-        ).astype(jnp.float32)
-
-    incoming = lax.fori_loop(0, seq_count - 1, relay_state, jnp.zeros_like(flat_state))
+    spikes = jnp.sum(spike_decay_level).astype(jnp.bfloat16)
+    shared = share(
+        jnp.concatenate(
+            [flat_state.astype(jnp.bfloat16), jnp.full(flat_state.shape, spikes, jnp.bfloat16)], 0
+        ),
+        seq_count,
+        3,
+    )
+    shard_level = (
+        -tokens * head_decay_speed[None, :]
+        - spike_position_step * shared[:, heads_dev, 0].astype(jnp.float32)[:, None]
+    )
+    seq_row = jnp.arange(seq_count)
+    reached = (seq_row[:, None] >= seq_row[None, :]).astype(jnp.float32)
+    until = jnp.sum(reached[:, :, None] * shard_level[None], axis=1)
+    before = until - shard_level
+    order = jnp.arange(seq_count)[:, None]
+    own_before = lax.dynamic_index_in_dim(before, seq_index, 0)
+    own_until = lax.dynamic_index_in_dim(until, seq_index, 0)
+    weight_before = jnp.exp(jnp.where(order < seq_index, own_before - until, -jnp.inf))
+    weight_after = jnp.exp(jnp.where(order > seq_index, before - own_until, -jnp.inf))
+    incoming = jnp.sum(
+        weight_before[:, :, None] * shared[:, :heads_dev].astype(jnp.float32), axis=0
+    )
     incoming = incoming.reshape(heads_dev, HEAD, STATE)
     outputs = jnp.concatenate(pieces, axis=0) + jnp.exp(cum_level)[:, :, None] * jnp.einsum(
         "tn,hpn->thp", c_float, incoming, precision=highest
@@ -148,54 +424,32 @@
         output_gradient.reshape(blocks_dev, BLOCK, slice_width),
         preferred_element_type=jnp.float32,
     ).astype(jnp.bfloat16)
-    h_full, g_full = (
-        lax.all_gather(h_pick, ("expert", "mp"), axis=2, tiled=True),
-        lax.all_gather(g_pick, ("expert", "mp"), axis=2, tiled=True),
-    )
-    h_block = narrow(h_full, exp_index, mp_index, half_width)
-    g_block = narrow(g_full, exp_index, mp_index, half_width)
-    h_all, g_all = (
-        lax.all_gather(h_block, "seq", axis=0, tiled=True),
-        lax.all_gather(g_block, "seq", axis=0, tiled=True),
-    )
     present = jnp.any(route_table == exp_index, axis=1)
-    slot_of = jnp.cumsum(present.astype(jnp.int32)) - 1
+    slot_of = jnp.sum(reached * present.astype(jnp.float32)[None, :], axis=1).astype(jnp.int32) - 1
     select = ((slot_of[None, :] == jnp.arange(slot_total)[:, None]) & present[None, :]).astype(
-        jnp.bfloat16
-    )
-    x_rows = compact(select, h_all, half_width)
-    g_rows = compact(select, g_all, half_width)
+        jnp.float32
+    )
+    sizes = (seq_count, exp_count, mp_count, slot_total)
+    x_rows, g_rows = route(select, h_pick, g_pick, sizes)
+    x_rows = x_rows.reshape(-1, half_width)
+    g_rows = g_rows.reshape(-1, half_width)
     up_local = expert_up_weight[0]
     down_local = expert_down_weight[0]
-    pre_act = lax.psum(
-        rounded(jnp.dot(x_rows, up_local, preferred_element_type=jnp.float32)).astype(jnp.bfloat16),
-        "mp",
-    ).astype(jnp.float32)
+    pre_part = jnp.dot(x_rows, up_local, preferred_element_type=jnp.float32).astype(jnp.bfloat16)
+    act_part = jnp.einsum(
+        "td,fd->tf", g_rows, down_local, preferred_element_type=jnp.float32
+    ).astype(jnp.bfloat16)
+    pre_act = pre_part.astype(jnp.float32) + swapped(pre_part).astype(jnp.float32)
     activation = jax.nn.silu(pre_act).astype(jnp.bfloat16)
     down_grad = jnp.einsum("tf,td->fd", activation, g_rows, preferred_element_type=jnp.float32)
-    act_grad = lax.psum(
-        rounded(
-            jnp.einsum("td,fd->tf", g_rows, down_local, preferred_element_type=jnp.float32)
-        ).astype(jnp.bfloat16),
-        "mp",
-    ).astype(jnp.float32)
+    act_grad = act_part.astype(jnp.float32) + swapped(act_part).astype(jnp.float32)
     sigmoid_pre = jax.nn.sigmoid(pre_act)
     pre_grad = (act_grad * sigmoid_pre * (1.0 + pre_act * (1.0 - sigmoid_pre))).astype(jnp.bfloat16)
     up_grad = jnp.einsum("td,tf->df", x_rows, pre_grad, preferred_element_type=jnp.float32)
     row_grad = jnp.einsum("tf,df->td", pre_grad, up_local, preferred_element_type=jnp.float32)
-    row_grad = row_grad.astype(jnp.bfloat16).reshape(slot_total, BLOCK, half_width)
-    spread_rows = jnp.einsum("js,jrf->srf", select, row_grad, preferred_element_type=jnp.float32)
-    back_rows = lax.psum_scatter(
-        spread_rows.reshape(BLOCK * lax.axis_size("seq"), half_width).astype(jnp.bfloat16),
-        "seq",
-        scatter_dimension=0,
-        tiled=True,
-    )
-    arrived = lax.all_gather(back_rows[None], ("expert", "mp"), axis=0, tiled=True)
-    halves = lax.dynamic_index_in_dim(
-        arrived.reshape(exp_count, mp_count, BLOCK, half_width), slice_half, 1, keepdims=False
-    )
-    returned = lax.dynamic_slice_in_dim(halves, my_slice % exp_count * slice_width, slice_width, 2)
+    returned = unroute(select, row_grad.astype(jnp.bfloat16), sizes).reshape(
+        exp_count, BLOCK, slice_width
+    )
     token_grad = jnp.einsum("eb,erf->brf", chosen, returned, preferred_element_type=jnp.float32)
     total_grad = output_gradient.astype(jnp.float32) + token_grad.reshape(tokens, slice_width)
     grad_view = total_grad.reshape(tokens, heads_dev, HEAD)
@@ -238,12 +492,14 @@
         )
     flat_adjoint = adjoint.reshape(heads_dev, HEAD * STATE)
 
-    def relay_adjoint(rounds, carried_in):
-        return from_behind(
-            (device_decay[:, None] * carried_in + flat_adjoint).astype(jnp.bfloat16), "seq", -1
-        ).astype(jnp.float32)
-
-    later_adjoint = lax.fori_loop(0, seq_count - 1, relay_adjoint, jnp.zeros_like(flat_adjoint))
+    shared_adjoint = share(
+        jnp.concatenate([flat_adjoint, jnp.zeros_like(flat_adjoint)], 0).astype(jnp.bfloat16),
+        seq_count,
+        4,
+    )
+    later_adjoint = jnp.sum(
+        weight_after[:, :, None] * shared_adjoint[:, :heads_dev].astype(jnp.float32), axis=0
+    )
     later_adjoint = later_adjoint.reshape(heads_dev, HEAD, STATE)
     scan_grad = jnp.concatenate(back_pieces, axis=0) + jnp.exp(cum_level[-1][None, :] - cum_level)[
         :, :, None

time: 403 us -> 242 us (0.60)
  waiting for transfers between devices: 200 us -> 3.18 us
  Pallas kernels: 0 us -> 87.9 us
  local copies, waits for them, and re-layouts: 36.8 us -> 18.7 us
  starting transfers between devices: 17.5 us -> 0.64 us
  between operations: 15.3 us -> 2.21 us
    all_gather x5 -> x0, waiting for transfers between devices: 122 us -> none  [the longest x1 47 us: per_device(): lax.all_gather(h_pick, ('expert', 'mp'), axis=2, tiled=True)]
    pallas_call x0 -> x4, Pallas kernels: none -> 87.9 us  [the longest x1 44 us: route(): pl.pallas_call(functools.partial(route_kernel, sizes), out_shape=(out, ou...]
    reduce_scatter x1 -> x0, waiting for transfers between devices: 36.5 us -> none  [per_device(): lax.psum_scatter(spread_rows.reshape(BLOCK * lax.axis_size('seq'), half_w...]
    psum x1 -> x0, waiting for transfers between devices: 23.4 us -> none  [per_device(): lax.psum(rounded(jnp.dot(x_rows, up_local, preferred_element_type=jnp.flo...]
    ppermute x6 -> x2, starting transfers between devices: 17.2 us -> 0.64 us  [swapped(): return lax.ppermute(value, 'mp', [(0, 1), (1, 0)])]
    ppermute x6 -> x2, waiting for transfers between devices: 18.5 us -> 3.18 us  [swapped(): return lax.ppermute(value, 'mp', [(0, 1), (1, 0)])]
    dot_general x2, matrix products: 4.81 us -> 18.8 us  [per_device(): jnp.einsum('hts,shp->thp', weight_high, x_span, preferred_element_type=jn...]
    dynamic_slice x5 -> x0, local copies, waits for them, and re-layouts: 10.5 us -> none  [the longest x4 9.12 us: narrow(): lax.dynamic_slice_in_dim(row_set, mp_index * half_width, half_width, 1)]
  transfers between devices with their start and end apart: 13 -> 2, of which waited for: 12 -> 1; matrix products, arithmetic and copies ran while one was open for 22% -> 3% of each run, Pallas kernels for 0% -> 0%
where the time goes in v1:
time: 242 us; the launch traced here: 240 us
  matrix products  109 us (45%)
  Pallas kernels  87.9 us (36%)
  local copies, waits for them, and re-layouts  18.7 us (8%)
  other arithmetic  18.4 us (8%)
  waiting for transfers between devices  3.18 us (1%)
    pallas_call x1, Pallas kernels, route(): pl.pallas_call(functools.partial(route_kernel, sizes), out_shape=(out, ou...  44 us
    pallas_call x1, Pallas kernels, unroute(): pl.pallas_call(functools.partial(unroute_kernel, sizes), out_shape=jax.Sh...  28.7 us
    dot_general x2, matrix products, per_device(): jnp.einsum('hts,shp->thp', weight_high, x_span, preferred_element_type=jn...  18.8 us
    pallas_call x2, Pallas kernels, share(): pl.pallas_call(functools.partial(share_kernel, n_seq), out_shape=jax.Shap...  15.2 us
    dot_general x1, matrix products, per_device(): jnp.einsum('tf,td->fd', activation, g_rows, preferred_element_type=jnp.fl...  10.9 us
    dot_general x1, matrix products, per_device(): jnp.einsum('td,tf->df', x_rows, pre_grad, preferred_element_type=jnp.floa...  10.8 us
    dot_general x1, matrix products, per_device(): jnp.einsum('td,fd->tf', g_rows, down_local, preferred_element_type=jnp.fl...  8.02 us
    dot_general x1, matrix products, per_device(): jnp.dot(x_rows, up_local, preferred_element_type=jnp.float32)  7.98 us
  transfers between devices with their start and end apart: 2, of which 1 were waited for; matrix products, arithmetic and copies ran while one was open for 3% of the time, Pallas kernels for 0%

profile of v1, /device:TPU:0, one launch (start us, length us, event | category | flops | bytes accessed | tf_op | source)
XLA Modules:
  0.0 240.3 jit_solution(8020518066916673865)
XLA Ops:
  0.6 0.6 fusion.141
  1.2 1.2 broadcast_multiply_fusion.2
  2.4 1.4 fusion.172
  3.8 0.5 fusion.50
  4.3 0.8 multiply_subtract_fusion
  5.3 1.3 subtract_exponential_fusion
  6.7 0.6 fusion.173
  7.5 2.1 fusion.136
  9.6 2.0 fusion.129
  11.6 0.9 fusion.171
  12.5 1.6 copy.109
  14.1 0.6 iota_compare_fusion.5
  15.7 0.7 convolution_convert_fusion
  16.6 2.0 copy.107
  18.6 1.0 copy.108
  19.6 4.0 %fusion.60 = f32[8,512,64]{1,2,0:T(8,128)S(1)} fusion(bf16[512,8,64]{0,2,1:T(8,128)(2,1)} %bitcast.155, f32[512,512]{1,0:T(8,128)} %fusion.129, f32[8,512]{1,0:T(8,128)S(1)} %get-tuple-element.22, pred[512,512]{1,0:T(8,128)(4,1)S(1)} %iota_compare_fusion.2), kind=kOutput, calls=%fused_computation.57 | convolution fusion | flops 283115520 | bytes 2899968 | tf_op jit(solution)/shard_map/hts,shp->thp/dot_general | solution.py:363
  23.7 3.4 %fusion.84 = f32[512,8,64]{0,2,1:T(8,128)} fusion(f32[8,512,64]{1,2,0:T(8,128)S(1)} %fusion.60, bf16[512,8,64]{0,2,1:T(8,128)(2,1)S(1)} %bitcast.156, f32[512,512]{1,0:T(8,128)S(1)} %copy-done.8, f32[8,512]{1,0:T(8,128)S(1)} %get-tuple-element.22, pred[512,512]{1,0:T(8,128)(4,1)S(1)} %iota_compare_fusion.2, f32[8]{0:T(128)S(1)} %get-tuple-element.32), kind=kOutput, calls=%fused_computation.89 | convolution fusion | flops 277348352 | bytes 3948576 | tf_op jit(solution)/shard_map/hts,shp->thp/dot_general | solution.py:360
  27.1 2.7 %fusion.58 = f32[8,512,64]{1,2,0:T(8,128)S(1)} fusion(bf16[512,8,64]{0,2,1:T(8,128)(2,1)S(1)} %bitcast.153, f32[512,512]{1,0:T(8,128)S(1)} %copy-done.10, f32[8,512]{1,0:T(8,128)S(1)} %get-tuple-element.21, pred[512,512]{1,0:T(8,128)(4,1)S(1)} %iota_compare_fusion.2), kind=kOutput, calls=%fused_computation.55 | convolution fusion | flops 283115520 | bytes 2899968 | tf_op jit(solution)/shard_map/hts,shp->thp/dot_general | solution.py:363
  29.8 15.4 %fusion.96 = f32[512,8,64]{0,2,1:T(8,128)} fusion(f32[8,512,64]{1,2,0:T(8,128)S(1)} %fusion.58, bf16[512,8,64]{0,2,1:T(8,128)(2,1)S(1)} %bitcast.154, f32[512,512]{1,0:T(8,128)S(1)} %copy-done.10, f32[8,512]{1,0:T(8,128)S(1)} %get-tuple-element.21, pred[512,512]{1,0:T(8,128)(4,1)S(1)} %iota_compare_fusion.2, f32[8]{0:T(128)S(1)} %get-tuple-element.32), kind=kOutput, calls=%fused_computation.93 | convolution fusion | flops 277348352 | bytes 3948576 | tf_op jit(solution)/shard_map/hts,shp->thp/dot_general | solution.py:360
  45.4 1.0 broadcast_multiply_fusion
  46.4 0.8 convolution_add_fusion.3
  47.2 0.8 fusion.102
  48.3 0.6 concatenate.13.x_ref
  48.9 8.2 %shard_map.112 = bf16[4,16,1024]{2,1,0:T(8,128)(2,1)} custom-call(bf16[16,1024]{1,0:T(8,128)(2,1)} %concatenate.13.x_ref), custom_call_target="tpu_custom_call" | custom-call | tf_op jit(solution)/shard_map/pallas_call | solution.py:57
  57.1 0.8 multiply_reduce_fusion.3
  58.3 0.9 multiply_reduce_fusion.1
  59.3 1.8 fusion.73
  61.1 1.9 fusion.71
  63.0 2.3 maximum_add_fusion
  65.3 2.9 %copy.112 = f32[1024,512]{1,0:T(8,128)} copy(f32[1024,512]{0,1:T(8,128)} %bitcast.142) | data formatting | bytes 4194304 | tf_op jit(solution)/shard_map/reshape | solution.py:408
  68.2 1.9 add_convert_fusion
  70.1 0.7 convolution_convert_fusion.1
  71.0 44.0 %shard_map.113 = (bf16[4,2,32,2048]{3,2,1,0:T(8,128)(2,1)S(1)}, bf16[4,2,32,2048]{3,2,1,0:T(8,128)(2,1)S(1)}) custom-call(f32[2,4]{1,0:T(2,128)S(1)} %and_convert_fusion.sel_ref, bf16[4,4,32,512]{3,2,1,0:T(8,128)(2,1)S(1)} %bitcast.133, bf16[4,4,32,512]{3,2,1,0:T(8,128)(2,1)S(1)} %bitcast.132), custom_call_target="tpu_custom_call" | custom-call | tf_op jit(solution)/shard_map/pallas_call | solution.py:187
  115.0 8.0 %fusion.51 = bf16[256,3072]{1,0:T(8,128)(2,1)S(1)} fusion(bf16[256,2048]{1,0:T(8,128)(2,1)S(1)} %bitcast.138, bf16[1,3072,2048]{2,1,0:T(8,128)(2,1)} %param.17), kind=kOutput, calls=%fused_computation.52 | convolution fusion | flops 3222011904 | bytes 15204352 | tf_op jit(solution)/shard_map/td,fd->tf/dot_general | solution.py:439
  123.0 0.3 collective-permute-start
  123.3 8.0 %fusion.54 = bf16[256,3072]{1,0:T(8,128)(2,1)S(1)} fusion(bf16[256,2048]{1,0:T(8,128)(2,1)S(1)} %bitcast.135, bf16[1,2048,3072]{2,1,0:T(8,128)(2,1)} %param.16), kind=kOutput, calls=%fused_computation.53 | convolution fusion | flops 3222011904 | bytes 15204352 | tf_op jit(solution)/shard_map/dot_general | solution.py:438
  131.6 3.2 %collective-permute-done.1 = bf16[256,3072]{1,0:T(8,128)(2,1)S(1)} collective-permute-done((bf16[256,3072]{1,0:T(8,128)(2,1)S(1)}, bf16[256,3072]{1,0:T(8,128)(2,1)S(1)}, u32[]{:S(2)}, u32[]{:S(2)}) %collective-permute-start.1) | collective-permute-done | bytes 1572896 | tf_op jit(solution)/shard_map/ppermute | solution.py:291
  134.8 1.6 multiply_convert_fusion.1
  136.4 6.6 %fusion.61 = bf16[256,2048]{1,0:T(8,128)(2,1)S(1)} fusion(bf16[256,3072]{1,0:T(8,128)(2,1)S(1)} %multiply_convert_fusion.1, bf16[1,2048,3072]{2,1,0:T(8,128)(2,1)} %param.16), kind=kOutput, calls=%fused_computation.62 | convolution fusion | flops 3221749760 | bytes 15204352 | tf_op jit(solution)/shard_map/tf,df->td/dot_general | solution.py:449
  143.0 10.8 %convolution_bitcast_fusion.1 = f32[1,2048,3072]{2,1,0:T(8,128)} fusion(bf16[256,2048]{1,0:T(8,128)(2,1)S(1)} %bitcast.136, bf16[256,3072]{1,0:T(8,128)(2,1)S(1)} %multiply_convert_fusion.1), kind=kOutput, calls=%fused_computation.1 | convolution fusion | flops 3221225472 | bytes 27787264 | tf_op jit(solution)/shard_map/td,tf->df/dot_general | solution.py:448
  153.8 28.7 %shard_map.114 = bf16[4,4,32,512]{3,2,1,0:T(8,128)(2,1)S(1)} custom-call(f32[2,4]{1,0:T(2,128)S(1)} %and_convert_fusion.sel_ref, bf16[4,2,32,2048]{3,2,1,0:T(8,128)(2,1)S(1)} %bitcast.137), custom_call_target="tpu_custom_call" | custom-call | tf_op jit(solution)/shard_map/pallas_call | solution.py:271
  182.5 0.6 fusion.108
  183.1 1.2 copy.118
  184.3 0.4 bitcast_add_fusion
  184.7 1.3 copy-done
  186.0 1.1 fusion.170
  187.5 3.5 %fusion.8 = f32[8,64,512]{2,1,0:T(8,128)S(1)} fusion(f32[512,512]{1,0:T(8,128)} %fusion.136, f32[8,512]{1,0:T(8,128)S(1)} %copy-done.22, pred[512,512]{1,0:T(8,128)(4,1)} %copy-done.17, f32[512,8,64]{0,2,1:T(8,128)S(1)} %bitcast.148), kind=kOutput, calls=%fused_computation.14 | convolution fusion | flops 277872640 | bytes 3424256 | tf_op jit(solution)/shard_map/hts,thp->shp/dot_general | solution.py:474
  191.1 2.3 fusion.99
  193.3 3.5 %fusion.77 = f32[512,8,64]{0,2,1:T(8,128)} fusion(f32[8,64,512]{2,1,0:T(8,128)S(1)} %fusion.99, f32[512,512]{1,0:T(8,128)S(1)} %copy-done.11, f32[8,512]{1,0:T(8,128)S(1)} %copy-done.22, pred[512,512]{1,0:T(8,128)(4,1)S(1)} %copy-done.18, f32[512,8,64]{0,2,1:T(8,128)S(1)} %bitcast.150), kind=kOutput, calls=%fused_computation.86 | convolution fusion | flops 283639808 | bytes 4472832 | tf_op jit(solution)/shard_map/hts,thp->shp/dot_general | solution.py:477
  196.8 1.6 copy.120
  198.4 4.4 %fusion.14 = f32[8,64,512]{2,1,0:T(8,128)} fusion(f32[512,512]{1,0:T(8,128)} %fusion.129, f32[8,512]{1,0:T(8,128)S(1)} %get-tuple-element.22, pred[512,512]{1,0:T(8,128)(4,1)} %copy-done.17, f32[512,8,64]{0,2,1:T(8,128)S(1)} %bitcast.144), kind=kOutput, calls=%fused_computation.17 | convolution fusion | flops 277872640 | bytes 3424256 | tf_op jit(solution)/shard_map/hts,thp->shp/dot_general | solution.py:474
  202.9 0.9 convolution_add_fusion.1
  203.8 0.8 fusion.103
  204.6 0.7 fusion.69
  205.6 0.6 concatenate.15.x_ref
  206.2 7.0 %shard_map.115 = bf16[4,16,1024]{2,1,0:T(8,128)(2,1)} custom-call(bf16[16,1024]{1,0:T(8,128)(2,1)} %concatenate.15.x_ref), custom_call_target="tpu_custom_call" | custom-call | tf_op jit(solution)/shard_map/pallas_call | solution.py:57
  213.3 0.9 multiply_reduce_fusion
  214.3 3.8 %fusion.87 = f32[8,64,512]{2,1,0:T(8,128)S(1)} fusion(f32[8,64,512]{2,1,0:T(8,128)} %fusion.14, f32[512,512]{1,0:T(8,128)} %fusion.129, f32[8,512]{1,0:T(8,128)S(1)} %get-tuple-element.22, pred[512,512]{1,0:T(8,128)(4,1)} %copy-done.17, f32[512,8,64]{0,2,1:T(8,128)S(1)} %bitcast.146), kind=kOutput, calls=%fused_computation.90 | convolution fusion | flops 277348352 | bytes 4472832 | tf_op jit(solution)/shard_map/hts,thp->shp/dot_general | solution.py:471
  218.2 2.5 %fusion.75 = f32[512,8,64]{0,2,1:T(8,128)S(1)} fusion(f32[8,64,512]{2,1,0:T(8,128)S(1)} %fusion.87, f32[512,512]{1,0:T(8,128)S(1)} %copy-done.9, f32[8,512]{1,0:T(8,128)S(1)} %get-tuple-element.22, pred[512,512]{1,0:T(8,128)(4,1)S(1)} %copy-done.19, f32[512,8,64]{0,2,1:T(8,128)S(1)} %bitcast.147), kind=kOutput, calls=%fused_computation.84 | convolution fusion | flops 283639808 | bytes 4472832 | tf_op jit(solution)/shard_map/hts,thp->shp/dot_general | solution.py:477
  220.7 0.6 fusion.67
  221.3 2.4 fusion.64
  223.7 1.9 copy.123
  225.7 3.5 %add.134 = f32[1024,512]{1,0:T(8,128)} add(f32[1024,512]{1,0:T(8,128)} %copy-done, f32[1024,512]{1,0:T(8,128)S(1)} %copy.123) | non-fusion elementwise | flops 524288 | bytes 6291456 | tf_op jit(solution)/shard_map/add | solution.py:507
  229.2 10.9 %convolution_bitcast_fusion = f32[1,3072,2048]{2,1,0:T(8,128)} fusion(bf16[256,2048]{1,0:T(8,128)(2,1)S(1)} %bitcast.139, bf16[256,3072]{1,0:T(8,128)(2,1)S(1)} %copy-done.7, bf16[256,3072]{1,0:T(8,128)(2,1)S(1)} %copy-done.5), kind=kOutput, calls=%fused_computation | convolution fusion | flops 3227516928 | bytes 29360128 | tf_op jit(solution)/shard_map/tf,td->fd/dot_general | solution.py:444
  (100 shorter events, 2.9 us)
Async XLA Ops:
  0.6 11.0 %copy-start.1 = (bf16[1024,512]{1,0:T(8,128)(2,1)S(1)}, bf16[1024,512]{1,0:T(8,128)(2,1)}, u32[]{:S(2)}) copy-start(bf16[1024,512]{1,0:T(8,128)(2,1)} %param.9) | copy-start | bytes 3145732
  2.4 27.4 %copy-start.26 = (f32[8]{0:T(128)}, f32[8]{0:T(128)S(1)}, u32[]{:S(2)}) copy-start(f32[8]{0:T(128)S(1)} %get-tuple-element.32) | copy-start | bytes 100
  4.3 10.4 %copy-start.33 = (s32[32]{0:T(128)S(1)}, s32[32]{0:T(128)}, u32[]{:S(2)}) copy-start(s32[32]{0:T(128)} %param.15) | copy-start | bytes 388
  4.3 11.4 %copy-start.3 = (bf16[1024,512]{1,0:T(8,128)(2,1)S(1)}, bf16[1024,512]{1,0:T(8,128)(2,1)}, u32[]{:S(2)}) copy-start(bf16[1024,512]{1,0:T(8,128)(2,1)} %param.10) | copy-start | bytes 3145732
  7.4 22.4 %copy-start.21 = (f32[8,512]{1,0:T(8,128)}, f32[8,512]{1,0:T(8,128)S(1)}, u32[]{:S(2)}) copy-start(f32[8,512]{1,0:T(8,128)S(1)} %get-tuple-element.21) | copy-start | bytes 49156
  7.5 22.3 %copy-start.17 = (pred[512,512]{1,0:T(8,128)(4,1)}, pred[512,512]{1,0:T(8,128)(4,1)S(1)}, u32[]{:S(2)}) copy-start(pred[512,512]{1,0:T(8,128)(4,1)S(1)} %iota_compare_fusion.2) | copy-start | bytes 786436
  14.9 8.7 %copy-start.24 = (s32[8]{0:T(128)}, s32[8]{0:T(128)S(1)}, u32[]{:S(2)}) copy-start(s32[8]{0:T(128)S(1)} %fusion.143) | copy-start | bytes 100
  19.6 4.0 %copy-start.8 = (f32[512,512]{1,0:T(8,128)S(1)}, f32[512,512]{1,0:T(8,128)}, u32[]{:S(2)}) copy-start(f32[512,512]{1,0:T(8,128)} %fusion.129) | copy-start | bytes 3145732
  19.6 4.0 %copy-start.16 = (bf16[512,512]{0,1:T(8,128)(2,1)S(1)}, bf16[512,512]{0,1:T(8,128)(2,1)}, u32[]{:S(2)}) copy-start(bf16[512,512]{0,1:T(8,128)(2,1)} %copy.108) | copy-start | bytes 1572868
  23.7 3.4 %copy-start.10 = (f32[512,512]{1,0:T(8,128)S(1)}, f32[512,512]{1,0:T(8,128)}, u32[]{:S(2)}) copy-start(f32[512,512]{1,0:T(8,128)} %fusion.136) | copy-start | bytes 3145732
  23.7 3.4 %copy-start.15 = (bf16[512,512]{0,1:T(8,128)(2,1)S(1)}, bf16[512,512]{0,1:T(8,128)(2,1)}, u32[]{:S(2)}) copy-start(bf16[512,512]{0,1:T(8,128)(2,1)} %copy.107) | copy-start | bytes 1572868
  29.8 15.6 %copy-start.2 = (f32[1024,512]{0,1:T(8,128)S(1)}, f32[1024,512]{0,1:T(8,128)}, u32[]{:S(2)}) copy-start(f32[1024,512]{0,1:T(8,128)} %copy.109) | copy-start | bytes 6291460
  45.3 1.1 copy-start.14
  45.3 1.1 copy-start.31
  45.3 1.9 copy-start.30
  45.3 12.6 %copy-start.32 = (f32[8]{0:T(128)S(1)}, f32[8]{0:T(128)}, u32[]{:S(2)}) copy-start(f32[8]{0:T(128)} %get-tuple-element.31) | copy-start | bytes 100
  45.3 12.7 %copy-start.23 = (f32[4,4]{1,0:T(4,128)S(1)}, f32[4,4]{1,0:T(4,128)}, u32[]{:S(2)}) copy-start(f32[4,4]{1,0:T(4,128)} %fusion.141) | copy-start | bytes 196
  45.3 12.7 %copy-start.35 = (pred[4]{0:T(512)(128)(4,1)S(1)}, pred[4]{0:T(512)(128)(4,1)}, u32[]{:S(2)}) copy-start(pred[4]{0:T(512)(128)(4,1)} %get-tuple-element.35) | copy-start | bytes 16
  45.3 12.8 %copy-start.34 = (pred[4]{0:T(512)(128)(4,1)S(1)}, pred[4]{0:T(512)(128)(4,1)}, u32[]{:S(2)}) copy-start(pred[4]{0:T(512)(128)(4,1)} %get-tuple-element.36) | copy-start | bytes 16
  45.4 14.0 %copy-start.13 = (bf16[1024,16]{0,1:T(8,128)(2,1)S(1)}, bf16[1024,16]{0,1:T(8,128)(2,1)}, u32[]{:S(2)}) copy-start(bf16[1024,16]{0,1:T(8,128)(2,1)} %param.12) | copy-start | bytes 98308
  46.4 16.6 %copy-start.20 = (f32[1024,8]{0,1:T(8,128)S(1)}, f32[1024,8]{0,1:T(8,128)}, u32[]{:S(2)}) copy-start(f32[1024,8]{0,1:T(8,128)} %get-tuple-element.24) | copy-start | bytes 98308
  65.3 4.8 %copy-start.25 = (s32[8]{0:T(128)S(1)}, s32[8]{0:T(128)}, u32[]{:S(2)}) copy-start(s32[8]{0:T(128)} %copy-done.24) | copy-start | bytes 100
  123.0 8.6 %collective-permute-start = (bf16[256,3072]{1,0:T(8,128)(2,1)S(1)}, bf16[256,3072]{1,0:T(8,128)(2,1)S(1)}, u32[]{:S(2)}, u32[]{:S(2)}) collective-permute-start(bf16[256,3072]{1,0:T(8,128)(2,1)S(1)} %fusion.51), channel_id=1, source_target_pairs={{0,1},{1,0},{2,3},{3,2},{4,5},{5,4},{6,7},{7,6},{8,9},{9,8},{10,11... | collective-permute-start | bytes 4718600 | tf_op jit(solution)/shard_map/ppermute | solution.py:291
  131.3 11.7 %copy-start.4 = (bf16[256,3072]{1,0:T(8,128)(2,1)}, bf16[256,3072]{1,0:T(8,128)(2,1)S(1)}, u32[]{:S(2)}) copy-start(bf16[256,3072]{1,0:T(8,128)(2,1)S(1)} %fusion.54) | copy-start | bytes 4718596
  131.3 3.5 %collective-permute-start.1 = (bf16[256,3072]{1,0:T(8,128)(2,1)S(1)}, bf16[256,3072]{1,0:T(8,128)(2,1)S(1)}, u32[]{:S(2)}, u32[]{:S(2)}) collective-permute-start(bf16[256,3072]{1,0:T(8,128)(2,1)S(1)} %fusion.54), channel_id=1, source_target_pairs={{0,1},{1,0},{2,3},{3,2},{4,5},{5,4},{6,7},{7,6},{8,9},{9,8},{10,11... | collective-permute-start | bytes 4718600 | tf_op jit(solution)/shard_map/ppermute | solution.py:291
  134.8 8.2 %copy-start.6 = (bf16[256,3072]{1,0:T(8,128)(2,1)}, bf16[256,3072]{1,0:T(8,128)(2,1)S(1)}, u32[]{:S(2)}) copy-start(bf16[256,3072]{1,0:T(8,128)(2,1)S(1)} %collective-permute-done.1) | copy-start | bytes 4718596
  184.7 1.3 copy-start
  186.0 1.5 copy-start.22
  187.5 3.5 %copy-start.11 = (f32[512,512]{1,0:T(8,128)S(1)}, f32[512,512]{1,0:T(8,128)}, u32[]{:S(2)}) copy-start(f32[512,512]{1,0:T(8,128)} %fusion.136) | copy-start | bytes 3145732
  187.5 3.5 %copy-start.18 = (pred[512,512]{1,0:T(8,128)(4,1)S(1)}, pred[512,512]{1,0:T(8,128)(4,1)}, u32[]{:S(2)}) copy-start(pred[512,512]{1,0:T(8,128)(4,1)} %copy-done.17) | copy-start | bytes 786436
  198.4 4.5 %copy-start.29 = (f32[8]{0:T(128)S(1)}, f32[8]{0:T(128)}, u32[]{:S(2)}) copy-start(f32[8]{0:T(128)} %get-tuple-element.29) | copy-start | bytes 100
  198.4 5.4 %copy-start.28 = (f32[8]{0:T(128)S(1)}, f32[8]{0:T(128)}, u32[]{:S(2)}) copy-start(f32[8]{0:T(128)} %get-tuple-element.27) | copy-start | bytes 100
  198.4 6.2 %copy-start.12 = (f32[512,8,64]{0,2,1:T(8,128)S(1)}, f32[512,8,64]{0,2,1:T(8,128)}, u32[]{:S(2)}) copy-start(f32[512,8,64]{0,2,1:T(8,128)} %fusion.77) | copy-start | bytes 3145732
  214.3 3.9 %copy-start.9 = (f32[512,512]{1,0:T(8,128)S(1)}, f32[512,512]{1,0:T(8,128)}, u32[]{:S(2)}) copy-start(f32[512,512]{1,0:T(8,128)} %fusion.129) | copy-start | bytes 3145732
  214.3 3.9 %copy-start.19 = (pred[512,512]{1,0:T(8,128)(4,1)S(1)}, pred[512,512]{1,0:T(8,128)(4,1)}, u32[]{:S(2)}) copy-start(pred[512,512]{1,0:T(8,128)(4,1)} %copy-done.17) | copy-start | bytes 786436
  218.2 3.2 %copy-start.27 = (f32[8]{0:T(128)S(1)}, f32[8]{0:T(128)}, u32[]{:S(2)}) copy-start(f32[8]{0:T(128)} %copy-done.26) | copy-start | bytes 100
  225.6 3.6 %copy-start.5 = (bf16[256,3072]{1,0:T(8,128)(2,1)S(1)}, bf16[256,3072]{1,0:T(8,128)(2,1)}, u32[]{:S(2)}) copy-start(bf16[256,3072]{1,0:T(8,128)(2,1)} %copy-done.4) | copy-start | bytes 4718596
  225.7 3.6 %copy-start.7 = (bf16[256,3072]{1,0:T(8,128)(2,1)S(1)}, bf16[256,3072]{1,0:T(8,128)(2,1)}, u32[]{:S(2)}) copy-start(bf16[256,3072]{1,0:T(8,128)(2,1)} %copy-done.6) | copy-start | bytes 4718596

commit v2 on v1

--- a/solution.py
+++ b/solution.py
@@ -12,7 +12,6 @@
 
 
 spike_position_step = 0.3
-highest = lax.Precision.HIGHEST
 
 
 MESH = pl.DeviceIdType.MESH
@@ -291,16 +290,77 @@
     return lax.ppermute(value, "mp", [(0, 1), (1, 0)])
 
 
-def split_parts(values):
-    high_part = values.astype(jnp.bfloat16)
-    low_part = (values - high_part.astype(jnp.float32)).astype(jnp.bfloat16)
-    return (high_part, low_part)
-
-
-def mixing(cum_block, scores, causal):
-    spread = cum_block.T[:, :, None] - cum_block.T[:, None, :]
-    spread = jnp.where(causal[None], spread, -jnp.inf)
-    return jnp.exp(spread) * scores[None]
+def contract(left, right, left_dim, right_dim):
+    return lax.dot_general(
+        left, right, (((left_dim,), (right_dim,)), ((), ())), preferred_element_type=jnp.float32
+    )
+
+
+def scan_kernel(reverse, speed_ref, x_ref, b_ref, c_ref, wide_ref, col_ref, row_ref, y_ref, state_ref):
+    blocks = x_ref.shape[0] // BLOCK
+    width = x_ref.shape[1]
+    step = lax.broadcasted_iota(jnp.int32, (BLOCK, 1), 0).astype(jnp.float32) + 1.0
+    later = lax.broadcasted_iota(jnp.int32, (BLOCK, BLOCK), 0)
+    earlier = lax.broadcasted_iota(jnp.int32, (BLOCK, BLOCK), 1)
+    causal = later >= earlier
+    gap = (later - earlier).astype(jnp.float32)
+    left_lane = lax.broadcasted_iota(jnp.int32, (BLOCK, 2 * HEAD), 1) < HEAD
+    state = jnp.zeros(state_ref.shape, jnp.float32)
+    for k in reversed(range(blocks)) if reverse else range(blocks):
+        rows = slice(k * BLOCK, (k + 1) * BLOCK)
+        spikes = col_ref[rows]
+        if k > 0:
+            since = spikes - col_ref[k * BLOCK - 1 : k * BLOCK]
+        else:
+            since = spikes
+        level = -step * wide_ref[...] - spike_position_step * since
+        end = level[BLOCK - 1 :]
+        b_now, c_now = b_ref[rows], c_ref[rows]
+        scores = contract(c_now, b_now, 1, 1)
+        spike_gap = spike_position_step * (spikes - row_ref[k : k + 1])
+        x_now = x_ref[rows].astype(jnp.float32)
+        from_start, to_end = jnp.exp(level), jnp.exp(end - level)
+        held = state.astype(jnp.bfloat16)
+        if reverse:
+            carried = to_end * contract(b_now, held, 1, 0)
+            added = contract(c_now, (x_now * from_start).astype(jnp.bfloat16), 0, 0)
+        else:
+            carried = from_start * contract(c_now, held, 1, 0)
+            added = contract(b_now, (x_now * to_end).astype(jnp.bfloat16), 0, 0)
+        state = jnp.exp(end) * state + added
+        for pair in range(width // (2 * HEAD)):
+            lanes = slice(pair * 2 * HEAD, (pair + 1) * 2 * HEAD)
+            x_pair = x_ref[rows, lanes].astype(jnp.bfloat16)
+            parts = []
+            for head in (2 * pair, 2 * pair + 1):
+                spread = jnp.where(causal, -gap * speed_ref[head] - spike_gap, -jnp.inf)
+                weights = (jnp.exp(spread) * scores).astype(jnp.bfloat16)
+                parts.append(contract(weights, x_pair, 0 if reverse else 1, 0))
+            y_ref[rows, lanes] = carried[:, lanes] + jnp.where(left_lane, parts[0], parts[1])
+    state_ref[...] = state
+
+
+def local_scan(reverse, speed, x, b, c, spike_count):
+    tokens, width = x.shape
+    vmem = pl.BlockSpec(memory_space=pltpu.VMEM)
+    return pl.pallas_call(
+        functools.partial(scan_kernel, reverse),
+        out_shape=(
+            jax.ShapeDtypeStruct((tokens, width), jnp.float32),
+            jax.ShapeDtypeStruct((STATE, width), jnp.float32),
+        ),
+        in_specs=[pl.BlockSpec(memory_space=pltpu.SMEM)] + [vmem] * 6,
+        out_specs=(vmem, vmem),
+        compiler_params=pltpu.CompilerParams(vmem_limit_bytes=40 * 2**20),
+    )(
+        speed,
+        x,
+        b,
+        c,
+        jnp.repeat(speed, HEAD)[None, :],
+        spike_count,
+        spike_count.reshape(tokens // BLOCK, BLOCK),
+    )
 
 
 def per_device(
@@ -315,7 +375,6 @@
     expert_down_weight,
 ):
     tokens, slice_width = activations.shape
-    heads_dev = slice_width // HEAD
     seq_count = lax.axis_size("seq")
     exp_count = lax.axis_size("expert")
     mp_count = lax.axis_size("mp")
@@ -330,53 +389,14 @@
         spike_decay_level.astype(jnp.bfloat16)[:, None],
         preferred_element_type=jnp.float32,
     )
+    wide_speed = jnp.repeat(head_decay_speed, HEAD)[None, :]
+    wide_scale = jnp.repeat(input_scale, HEAD)[None, :]
     cum_level = (
-        -(row + 1).astype(jnp.float32)[:, None] * head_decay_speed[None, :]
-        - spike_position_step * spike_count
-    )
-    b_float = input_state_map.astype(jnp.float32)
-    c_float = output_state_map.astype(jnp.float32)
-    act_heads = activations.reshape(tokens, heads_dev, HEAD)
-    scaled = act_heads.astype(jnp.float32) * input_scale[None, :, None]
-    span_rows = min(512, tokens)
-    span_count = tokens // span_rows
-    causal = jnp.arange(span_rows)[:, None] >= jnp.arange(span_rows)[None, :]
-    zero_level = jnp.zeros((heads_dev,), jnp.float32)
-    carry_state = jnp.zeros((heads_dev, HEAD, STATE), jnp.float32)
-    pieces = []
-    for position in range(span_count):
-        first_row = position * span_rows
-        last_row = first_row + span_rows
-        cum_block = cum_level[first_row:last_row]
-        start_level = cum_level[first_row - 1] if position > 0 else zero_level
-        scores = jnp.dot(
-            output_state_map[first_row:last_row],
-            input_state_map[first_row:last_row].T,
-            preferred_element_type=jnp.float32,
-        )
-        weights = mixing(cum_block, scores, causal)
-        weight_high, weight_low = split_parts(weights)
-        x_span = act_heads[first_row:last_row]
-        inner_part = jnp.einsum(
-            "hts,shp->thp", weight_high, x_span, preferred_element_type=jnp.float32
-        )
-        inner_part = inner_part + jnp.einsum(
-            "hts,shp->thp", weight_low, x_span, preferred_element_type=jnp.float32
-        )
-        inner_part = inner_part * input_scale[None, :, None]
-        carried = jnp.exp(cum_block - start_level[None, :])[:, :, None] * jnp.einsum(
-            "tn,hpn->thp", c_float[first_row:last_row], carry_state, precision=highest
-        )
-        pieces.append(inner_part + carried)
-        end_level = cum_block[-1]
-        tail_decay = jnp.exp(end_level[None, :] - cum_block)
-        carry_state = jnp.exp(end_level - start_level)[:, None, None] * carry_state + jnp.einsum(
-            "shp,sn->hpn",
-            scaled[first_row:last_row] * tail_decay[:, :, None],
-            b_float[first_row:last_row],
-            precision=highest,
-        )
-    flat_state = carry_state.reshape(heads_dev, HEAD * STATE)
+        -(row + 1).astype(jnp.float32)[:, None] * wide_speed - spike_position_step * spike_count
+    )
+    scan_local, flat_state = local_scan(
+        False, head_decay_speed, activations, input_state_map, output_state_map, spike_count
+    )
     spikes = jnp.sum(spike_decay_level).astype(jnp.bfloat16)
     shared = share(
         jnp.concatenate(
@@ -386,8 +406,8 @@
         3,
     )
     shard_level = (
-        -tokens * head_decay_speed[None, :]
-        - spike_position_step * shared[:, heads_dev, 0].astype(jnp.float32)[:, None]
+        -tokens * wide_speed
+        - spike_position_step * shared[:, STATE, 0].astype(jnp.float32)[:, None]
     )
     seq_row = jnp.arange(seq_count)
     reached = (seq_row[:, None] >= seq_row[None, :]).astype(jnp.float32)
@@ -399,15 +419,12 @@
     weight_before = jnp.exp(jnp.where(order < seq_index, own_before - until, -jnp.inf))
     weight_after = jnp.exp(jnp.where(order > seq_index, before - own_until, -jnp.inf))
     incoming = jnp.sum(
-        weight_before[:, :, None] * shared[:, :heads_dev].astype(jnp.float32), axis=0
-    )
-    incoming = incoming.reshape(heads_dev, HEAD, STATE)
-    outputs = jnp.concatenate(pieces, axis=0) + jnp.exp(cum_level)[:, :, None] * jnp.einsum(
-        "tn,hpn->thp", c_float, incoming, precision=highest
-    )
-    mixed_out = (activations.astype(jnp.float32) + outputs.reshape(tokens, slice_width)).astype(
-        jnp.bfloat16
-    )
+        weight_before[:, None, :] * shared[:, :STATE].astype(jnp.float32), axis=0
+    )
+    outputs = scan_local + jnp.exp(cum_level) * jnp.dot(
+        output_state_map, incoming.astype(jnp.bfloat16), preferred_element_type=jnp.float32
+    )
+    mixed_out = (activations.astype(jnp.float32) + wide_scale * outputs).astype(jnp.bfloat16)
     blocks_dev = tokens // BLOCK
     route_table = assign.reshape(seq_count, blocks_dev)
     own_row = lax.dynamic_index_in_dim(route_table, seq_index, 0, keepdims=False)
@@ -452,59 +469,21 @@
     )
     token_grad = jnp.einsum("eb,erf->brf", chosen, returned, preferred_element_type=jnp.float32)
     total_grad = output_gradient.astype(jnp.float32) + token_grad.reshape(tokens, slice_width)
-    grad_view = total_grad.reshape(tokens, heads_dev, HEAD)
-    adjoint = jnp.zeros((heads_dev, HEAD, STATE), jnp.float32)
-    back_pieces = [None] * span_count
-    for position in reversed(range(span_count)):
-        first_row = position * span_rows
-        last_row = first_row + span_rows
-        cum_block = cum_level[first_row:last_row]
-        start_level = cum_level[first_row - 1] if position > 0 else zero_level
-        scores = jnp.dot(
-            output_state_map[first_row:last_row],
-            input_state_map[first_row:last_row].T,
-            preferred_element_type=jnp.float32,
-        )
-        weights = mixing(cum_block, scores, causal)
-        weight_high, weight_low = split_parts(weights)
-        grad_high, grad_low = split_parts(grad_view[first_row:last_row])
-        inner_part = jnp.einsum(
-            "hts,thp->shp", weight_high, grad_high, preferred_element_type=jnp.float32
-        )
-        inner_part = inner_part + jnp.einsum(
-            "hts,thp->shp", weight_high, grad_low, preferred_element_type=jnp.float32
-        )
-        inner_part = inner_part + jnp.einsum(
-            "hts,thp->shp", weight_low, grad_high, preferred_element_type=jnp.float32
-        )
-        end_level = cum_block[-1]
-        tail_decay = jnp.exp(end_level[None, :] - cum_block)
-        carried = tail_decay[:, :, None] * jnp.einsum(
-            "sn,hpn->shp", b_float[first_row:last_row], adjoint, precision=highest
-        )
-        back_pieces[position] = inner_part + carried
-        lead_decay = jnp.exp(cum_block - start_level[None, :])
-        adjoint = jnp.exp(end_level - start_level)[:, None, None] * adjoint + jnp.einsum(
-            "rhp,rn->hpn",
-            grad_view[first_row:last_row] * lead_decay[:, :, None],
-            c_float[first_row:last_row],
-            precision=highest,
-        )
-    flat_adjoint = adjoint.reshape(heads_dev, HEAD * STATE)
-
+    adjoint_local, flat_adjoint = local_scan(
+        True, head_decay_speed, total_grad, input_state_map, output_state_map, spike_count
+    )
     shared_adjoint = share(
-        jnp.concatenate([flat_adjoint, jnp.zeros_like(flat_adjoint)], 0).astype(jnp.bfloat16),
+        flat_adjoint.astype(jnp.bfloat16),
         seq_count,
         4,
     )
     later_adjoint = jnp.sum(
-        weight_after[:, :, None] * shared_adjoint[:, :heads_dev].astype(jnp.float32), axis=0
-    )
-    later_adjoint = later_adjoint.reshape(heads_dev, HEAD, STATE)
-    scan_grad = jnp.concatenate(back_pieces, axis=0) + jnp.exp(cum_level[-1][None, :] - cum_level)[
-        :, :, None
-    ] * jnp.einsum("sn,hpn->shp", b_float, later_adjoint, precision=highest)
-    grad_x = total_grad + (input_scale[None, :, None] * scan_grad).reshape(tokens, slice_width)
+        weight_after[:, None, :] * shared_adjoint.astype(jnp.float32), axis=0
+    )
+    scan_grad = adjoint_local + jnp.exp(cum_level[-1:] - cum_level) * jnp.dot(
+        input_state_map, later_adjoint.astype(jnp.bfloat16), preferred_element_type=jnp.float32
+    )
+    grad_x = total_grad + wide_scale * scan_grad
     return (grad_x, up_grad[None], down_grad[None])
 
 

time: 242 us -> 170 us (0.70)
  matrix products: 109 us -> 53.6 us
  other arithmetic: 18.4 us -> 8.2 us
  local copies, waits for them, and re-layouts: 18.7 us -> 8.68 us
  Pallas kernels: 87.9 us -> 93.2 us
    dot_general x22 -> x2, matrix products: 62.6 us -> 6.42 us  [the longest x1 3.98 us: per_device(): jnp.dot(input_state_map, later_adjoint.astype(jnp.bfloat16), preferred_el...]
    slice x7 -> x1, local copies, waits for them, and re-layouts: 7.15 us -> 0.01 us  [per_device(): cum_level[-1:] - cum_level]
    pallas_call x0 -> x2, Pallas kernels: none -> 6.44 us  [local_scan(): pl.pallas_call(functools.partial(scan_kernel, reverse), out_shape=(jax.Sh...]
    reshape x5 -> x0, local copies, waits for them, and re-layouts: 5.22 us -> none  [the longest x1 2.88 us: per_device(): outputs.reshape(tokens, slice_width)]
    add x1 -> x0, other arithmetic: 3.55 us -> none  [per_device(): total_grad + (input_scale[None, :, None] * scan_grad).reshape(tokens, sli...]
    unnamed x72 -> x30, local copies, waits for them, and re-layouts: 1.49 us -> 4.63 us
  transfers between devices with their start and end apart: 2 -> 2, of which waited for: 1 -> 1; matrix products, arithmetic and copies ran while one was open for 3% -> 5% of each run, Pallas kernels for 0% -> 0%
where the time goes in v2:
time: 170 us; the launch traced here: 169 us
  Pallas kernels  93.2 us (55%)
  matrix products  53.6 us (32%)
  local copies, waits for them, and re-layouts  8.68 us (5%)
  other arithmetic  8.2 us (5%)
  waiting for transfers between devices  2.8 us (2%)
    pallas_call x1, Pallas kernels, route(): pl.pallas_call(functools.partial(route_kernel, sizes), out_shape=(out, ou...  44 us
    pallas_call x1, Pallas kernels, unroute(): pl.pallas_call(functools.partial(unroute_kernel, sizes), out_shape=jax.Sh...  28.5 us
    pallas_call x2, Pallas kernels, share(): pl.pallas_call(functools.partial(share_kernel, n_seq), out_shape=jax.Shap...  14.3 us
    dot_general x1, matrix products, per_device(): jnp.einsum('tf,td->fd', activation, g_rows, preferred_element_type=jnp.fl...  10.9 us
    dot_general x1, matrix products, per_device(): jnp.einsum('td,tf->df', x_rows, pre_grad, preferred_element_type=jnp.floa...  10.8 us
    dot_general x1, matrix products, per_device(): jnp.einsum('td,fd->tf', g_rows, down_local, preferred_element_type=jnp.fl...  8.4 us
    dot_general x1, matrix products, per_device(): jnp.dot(x_rows, up_local, preferred_element_type=jnp.float32)  8.04 us
    dot_general x1, matrix products, per_device(): jnp.einsum('tf,df->td', pre_grad, up_local, preferred_element_type=jnp.fl...  6.59 us
  transfers between devices with their start and end apart: 2, of which 1 were waited for; matrix products, arithmetic and copies ran while one was open for 5% of the time, Pallas kernels for 0%

profile of v2, /device:TPU:0, one launch (start us, length us, event | category | flops | bytes accessed | tf_op | source)
XLA Modules:
  0.0 168.8 jit_solution(12309481655352845615)
XLA Ops:
  0.6 0.0 copy-start.6
  0.7 0.8 subtract_sqrt_fusion
  1.4 0.7 broadcast_in_dim.27
  2.1 0.1 mul.125
  2.2 0.1 broadcast_in_dim_reshape.2.wide_ref
  2.3 0.7 reshape.210
  3.0 0.1 compare_reduce_fusion
  3.2 0.1 select_reduce_fusion
  3.3 1.4 fusion.39
  5.4 0.5 fusion.6
  5.8 0.1 broadcast_in_dim.26
  5.9 0.1 mul.122
  6.0 1.0 copy.38.b_ref
  7.0 0.9 copy.39.c_ref
  8.0 0.2 copy.40.col_ref
  8.2 0.0 copy-done.6
  8.2 0.7 convolution_convert_fusion
  9.0 0.0 copy-start.13
  9.0 0.1 copy.45
  9.1 0.0 copy-done.1
  9.1 0.0 copy-done.2
  9.1 3.1 %shard_map.112 = (f32[1024,512]{1,0:T(8,128)S(1)}, f32[16,512]{1,0:T(8,128)S(1)}) custom-call(f32[8]{0:T(128)S(1)} %copy-done.2, bf16[1024,512]{1,0:T(8,128)(2,1)S(1)} %copy-done.1, bf16[1024,16]{1,0:T(8,128)(2,1)S(1)} %copy.38.b_ref, bf16[1024,16]{1,0:T(8,128)(2,1)S(1)} %copy.39.c_ref, f32[1,512]{1,0:T(1,128)S(1)} %broadcast_in_dim_reshape.2.wide_ref, ...), custom_call_target="tpu_custom_call" | custom-call | tf_op jit(solution)/shard_map/pallas_call | solution.py:346
  12.2 0.0 copy-start.3
  12.3 1.3 copy-done.3
  13.6 0.6 concatenate.3.x_ref
  14.2 8.2 %shard_map.113 = bf16[4,32,512]{2,1,0:T(8,128)(2,1)} custom-call(bf16[32,512]{1,0:T(8,128)(2,1)} %concatenate.3.x_ref), custom_call_target="tpu_custom_call" | custom-call | tf_op jit(solution)/shard_map/pallas_call | solution.py:56
  22.4 0.8 multiply_reduce_fusion.3
  23.2 0.1 broadcast_subtract_fusion
  23.2 0.1 multiply_reduce_fusion.2
  23.4 0.1 select_exponential_fusion
  23.5 0.1 select_exponential_fusion.1
  23.5 0.9 multiply_reduce_fusion.1
  24.4 0.0 copy-done.13
  24.4 2.4 %fusion.22 = bf16[1024,512]{1,0:T(8,128)(2,1)S(1)} fusion(f32[1024,512]{1,0:T(8,128)} %copy-done.3, bf16[1024,512]{1,0:T(8,128)(2,1)S(1)} %copy-done.1, bf16[1024,16]{0,1:T(8,128)(2,1)S(1)} %copy-done.13, f32[1024]{0:T(1024)S(1)} %get-tuple-element.22, f32[512]{0:T(512)S(1)} %mul.125, f32[1024]{0:T(1024)S(1)} %get-tuple-element.21, f32[512]{0:T(512)S(1)} %mul.122, ...), kind=kOutput, calls=%fused_computation.26 | convolution fusion | flops 20971520 | bytes 4255744 | tf_op jit(solution)/shard_map/dot_general | solution.py:424
  26.9 0.7 convolution_convert_fusion.1
  27.6 0.1 copy.43
  27.7 44.0 %shard_map.114 = (bf16[4,2,32,2048]{3,2,1,0:T(8,128)(2,1)S(1)}, bf16[4,2,32,2048]{3,2,1,0:T(8,128)(2,1)S(1)}) custom-call(f32[2,4]{1,0:T(2,128)S(1)} %and_convert_fusion.sel_ref, bf16[4,4,32,512]{3,2,1,0:T(8,128)(2,1)S(1)} %bitcast.72, bf16[4,4,32,512]{3,2,1,0:T(8,128)(2,1)S(1)} %bitcast.71), custom_call_target="tpu_custom_call" | custom-call | tf_op jit(solution)/shard_map/pallas_call | solution.py:186
  71.7 0.0 copy-start.4
  71.7 8.4 %fusion.7 = bf16[256,3072]{1,0:T(8,128)(2,1)S(1)} fusion(bf16[256,2048]{1,0:T(8,128)(2,1)S(1)} %bitcast.81, bf16[1,3072,2048]{2,1,0:T(8,128)(2,1)} %param.17), kind=kOutput, calls=%fused_computation.10 | convolution fusion | flops 3222011904 | bytes 15204352 | tf_op jit(solution)/shard_map/td,fd->tf/dot_general | solution.py:456
  80.2 0.0 copy-done.4
  80.2 0.3 collective-permute-start
  80.5 8.0 %fusion.10 = bf16[256,3072]{1,0:T(8,128)(2,1)S(1)} fusion(bf16[256,2048]{1,0:T(8,128)(2,1)S(1)} %bitcast.74, bf16[1,2048,3072]{2,1,0:T(8,128)(2,1)} %param.16), kind=kOutput, calls=%fused_computation.11 | convolution fusion | flops 3222011904 | bytes 15204352 | tf_op jit(solution)/shard_map/dot_general | solution.py:455
  88.5 0.3 collective-permute-start.1
  88.9 0.3 multiply_subtract_fusion
  89.2 0.0 collective-permute-done
  89.2 2.8 %collective-permute-done.1 = bf16[256,3072]{1,0:T(8,128)(2,1)S(1)} collective-permute-done((bf16[256,3072]{1,0:T(8,128)(2,1)S(1)}, bf16[256,3072]{1,0:T(8,128)(2,1)S(1)}, u32[]{:S(2)}, u32[]{:S(2)}) %collective-permute-start.1) | collective-permute-done | bytes 1572896 | tf_op jit(solution)/shard_map/ppermute | solution.py:290
  92.0 1.6 multiply_convert_fusion.1
  93.7 6.6 %fusion.13 = bf16[256,2048]{1,0:T(8,128)(2,1)S(1)} fusion(bf16[256,3072]{1,0:T(8,128)(2,1)S(1)} %multiply_convert_fusion.1, bf16[1,2048,3072]{2,1,0:T(8,128)(2,1)} %param.16), kind=kOutput, calls=%fused_computation.16 | convolution fusion | flops 3221749760 | bytes 15204352 | tf_op jit(solution)/shard_map/tf,df->td/dot_general | solution.py:466
  100.3 10.8 %convolution_bitcast_fusion.1 = f32[1,2048,3072]{2,1,0:T(8,128)} fusion(bf16[256,2048]{1,0:T(8,128)(2,1)S(1)} %bitcast.75, bf16[256,3072]{1,0:T(8,128)(2,1)S(1)} %multiply_convert_fusion.1), kind=kOutput, calls=%fused_computation.1 | convolution fusion | flops 3221225472 | bytes 27787264 | tf_op jit(solution)/shard_map/td,tf->df/dot_general | solution.py:465
  111.0 28.5 %shard_map.115 = bf16[4,4,32,512]{3,2,1,0:T(8,128)(2,1)S(1)} custom-call(f32[2,4]{1,0:T(2,128)S(1)} %and_convert_fusion.sel_ref, bf16[4,2,32,2048]{3,2,1,0:T(8,128)(2,1)S(1)} %bitcast.76), custom_call_target="tpu_custom_call" | custom-call | tf_op jit(solution)/shard_map/pallas_call | solution.py:270
  139.6 0.6 fusion.26
  140.1 0.0 copy-start.7
  140.2 1.2 copy.47
  141.4 0.3 bitcast_add_fusion.x_ref
  141.7 0.0 copy-start.12
  141.8 3.3 %shard_map.116 = (f32[1024,512]{1,0:T(8,128)S(1)}, f32[16,512]{1,0:T(8,128)S(1)}) custom-call(f32[8]{0:T(128)S(1)} %copy-done.2, f32[1024,512]{1,0:T(8,128)S(1)} %bitcast_add_fusion.x_ref, bf16[1024,16]{1,0:T(8,128)(2,1)S(1)} %copy.38.b_ref, bf16[1024,16]{1,0:T(8,128)(2,1)S(1)} %copy.39.c_ref, f32[1,512]{1,0:T(1,128)S(1)} %broadcast_in_dim_reshape.2.wide_ref, ...), custom_call_target="tpu_custom_call" | custom-call | tf_op jit(solution)/shard_map/pallas_call | solution.py:346
  145.0 0.0 copy-start
  145.1 1.3 copy-done
  146.4 0.6 convert_element_type.131.x_ref
  147.0 6.1 %shard_map.117 = bf16[4,16,512]{2,1,0:T(8,128)(2,1)} custom-call(bf16[16,512]{1,0:T(8,128)(2,1)} %convert_element_type.131.x_ref), custom_call_target="tpu_custom_call" | custom-call | tf_op jit(solution)/shard_map/pallas_call | solution.py:56
  153.1 0.9 multiply_reduce_fusion
  154.0 0.0 copy-start.11
  154.0 4.0 %fusion.18 = f32[1024,512]{1,0:T(8,128)} fusion(f32[1024,512]{1,0:T(8,128)S(1)} %bitcast_add_fusion.x_ref, f32[1024,512]{1,0:T(8,128)} %copy-done, bf16[1024,16]{0,1:T(8,128)(2,1)S(1)} %copy-done.12, f32[512]{0:T(512)S(1)} %bitcast.85, f32[1024]{0:T(1024)S(1)} %get-tuple-element.22, f32[512]{0:T(512)S(1)} %mul.125, f32[1024]{0:T(1024)S(1)} %get-tuple-element.21, ...), kind=kOutput, calls=%fused_computation.20 | convolution fusion | flops 20447232 | bytes 6354944 | tf_op jit(solution)/shard_map/dot_general | solution.py:483
  158.0 10.9 %convolution_bitcast_fusion = f32[1,3072,2048]{2,1,0:T(8,128)} fusion(bf16[256,2048]{1,0:T(8,128)(2,1)S(1)} %bitcast.82, bf16[256,3072]{1,0:T(8,128)(2,1)S(1)} %copy-done.11, bf16[256,3072]{1,0:T(8,128)(2,1)S(1)} %copy-done.9), kind=kOutput, calls=%fused_computation | convolution fusion | flops 3227516928 | bytes 29360128 | tf_op jit(solution)/shard_map/tf,td->fd/dot_general | solution.py:461
  (26 shorter events, 0.1 us)
Async XLA Ops:
  0.6 7.6 %copy-start.6 = (bf16[1024,512]{1,0:T(8,128)(2,1)S(1)}, bf16[1024,512]{1,0:T(8,128)(2,1)}, u32[]{:S(2)}) copy-start(bf16[1024,512]{1,0:T(8,128)(2,1)} %param.10) | copy-start | bytes 3145732
  5.8 3.2 %copy-start.1 = (bf16[1024,512]{1,0:T(8,128)(2,1)S(1)}, bf16[1024,512]{1,0:T(8,128)(2,1)}, u32[]{:S(2)}) copy-start(bf16[1024,512]{1,0:T(8,128)(2,1)} %x_ref.1) | copy-start | bytes 3145732
  5.8 3.2 %copy-start.2 = (f32[8]{0:T(128)S(1)}, f32[8]{0:T(128)}, u32[]{:S(2)}) copy-start(f32[8]{0:T(128)} %speed_ref.3) | copy-start | bytes 100
  9.0 15.5 %copy-start.13 = (bf16[1024,16]{0,1:T(8,128)(2,1)S(1)}, bf16[1024,16]{0,1:T(8,128)(2,1)}, u32[]{:S(2)}) copy-start(bf16[1024,16]{0,1:T(8,128)(2,1)} %param.12) | copy-start | bytes 98308
  12.2 1.3 copy-start.3
  71.7 8.4 %copy-start.4 = (bf16[4,2,32,2048]{3,2,1,0:T(8,128)(2,1)}, bf16[4,2,32,2048]{3,2,1,0:T(8,128)(2,1)S(1)}, u32[]{:S(2)}) copy-start(bf16[4,2,32,2048]{3,2,1,0:T(8,128)(2,1)S(1)} %get-tuple-element.11) | copy-start | bytes 3145732
  80.2 9.1 %collective-permute-start = (bf16[256,3072]{1,0:T(8,128)(2,1)S(1)}, bf16[256,3072]{1,0:T(8,128)(2,1)S(1)}, u32[]{:S(2)}, u32[]{:S(2)}) collective-permute-start(bf16[256,3072]{1,0:T(8,128)(2,1)S(1)} %fusion.7), channel_id=1, source_target_pairs={{0,1},{1,0},{2,3},{3,2},{4,5},{5,4},{6,7},{7,6},{8,9},{9,8},{10,11... | collective-permute-start | bytes 4718600 | tf_op jit(solution)/shard_map/ppermute | solution.py:290
  88.5 5.1 %copy-start.8 = (bf16[256,3072]{1,0:T(8,128)(2,1)}, bf16[256,3072]{1,0:T(8,128)(2,1)S(1)}, u32[]{:S(2)}) copy-start(bf16[256,3072]{1,0:T(8,128)(2,1)S(1)} %fusion.10) | copy-start | bytes 4718596
  88.5 3.5 %collective-permute-start.1 = (bf16[256,3072]{1,0:T(8,128)(2,1)S(1)}, bf16[256,3072]{1,0:T(8,128)(2,1)S(1)}, u32[]{:S(2)}, u32[]{:S(2)}) collective-permute-start(bf16[256,3072]{1,0:T(8,128)(2,1)S(1)} %fusion.10), channel_id=1, source_target_pairs={{0,1},{1,0},{2,3},{3,2},{4,5},{5,4},{6,7},{7,6},{8,9},{9,8},{10,11... | collective-permute-start | bytes 4718600 | tf_op jit(solution)/shard_map/ppermute | solution.py:290
  92.0 1.6 copy-start.10
  140.1 1.2 copy-start.7
  141.7 12.2 %copy-start.12 = (bf16[1024,16]{0,1:T(8,128)(2,1)S(1)}, bf16[1024,16]{0,1:T(8,128)(2,1)}, u32[]{:S(2)}) copy-start(bf16[1024,16]{0,1:T(8,128)(2,1)} %param.11) | copy-start | bytes 98308
  145.0 1.3 copy-start
  153.9 4.0 %copy-start.5 = (bf16[4,2,32,2048]{3,2,1,0:T(8,128)(2,1)S(1)}, bf16[4,2,32,2048]{3,2,1,0:T(8,128)(2,1)}, u32[]{:S(2)}) copy-start(bf16[4,2,32,2048]{3,2,1,0:T(8,128)(2,1)} %copy-done.4) | copy-start | bytes 3145732
  153.9 4.0 %copy-start.9 = (bf16[256,3072]{1,0:T(8,128)(2,1)S(1)}, bf16[256,3072]{1,0:T(8,128)(2,1)}, u32[]{:S(2)}) copy-start(bf16[256,3072]{1,0:T(8,128)(2,1)} %copy-done.8) | copy-start | bytes 4718596
  154.0 4.0 %copy-start.11 = (bf16[256,3072]{1,0:T(8,128)(2,1)S(1)}, bf16[256,3072]{1,0:T(8,128)(2,1)}, u32[]{:S(2)}) copy-start(bf16[256,3072]{1,0:T(8,128)(2,1)} %copy-done.10) | copy-start | bytes 4718596
